TPU v7x, 128 devices: a whole 4x4x4 slice. The times are simulated.
128 devices in a mesh: dp: 32 (over x, y_lo, z), shard: 4 (over y_hi, core).
Axes of the slice: x: 4, y: 4 (y_hi: 2, y_lo: 2; y = y_hi * 2 + y_lo), z: 4, core: 2. Of those that a mesh axis runs over, the one named last changes fastest.
Arguments:
- tokens: bfloat16 [32768, 768], P(('dp', 'shard')), may hold values from -6 to 6
- bounds: int32 [32, 2], P('dp'), may hold values from 0 to 1024, as said below
- routes: int32 [32768, 2], P(('dp', 'shard')), may hold values from 0 to 63, all different within a row; in each aligned block of 256 rows (0 to 255, 256 to 511, ...) at most 16 rows name the same one
- ln1_gain: bfloat16 [768], P(('dp', 'shard')), may hold values from 0.099609375 to 1.8984375
- ln1_bias: bfloat16 [768], P(('dp', 'shard')), may hold values from -1.5 to 1.5
- query_weight: bfloat16 [768, 768], P(('dp', 'shard')), may hold values from -0.21875 to 0.21875
- key_weight: bfloat16 [768, 768], P(('dp', 'shard')), may hold values from -0.21875 to 0.21875
- value_weight: bfloat16 [768, 768], P(('dp', 'shard')), may hold values from -0.21875 to 0.21875
- output_weight: bfloat16 [768, 768], P(('dp', 'shard')), may hold values from -1.75 to 1.75
- ln2_gain: bfloat16 [768], P(('dp', 'shard')), may hold values from 0.099609375 to 1.8984375
- ln2_bias: bfloat16 [768], P(('dp', 'shard')), may hold values from -1.5 to 1.5
- gate_new: bfloat16 [768, 32], P(('dp', 'shard')), may hold values from -0.15625 to 0.15625
- gate_frozen: bfloat16 [768, 32], P(('dp', 'shard')), may hold values from -0.15625 to 0.15625
- new_in: bfloat16 [32, 768, 3072], P('dp', None, 'shard'), may hold values from -0.21875 to 0.21875
- new_out: bfloat16 [32, 3072, 768], P('dp', 'shard'), may hold values from -0.109375 to 0.109375
- frozen_in: bfloat16 [32, 768, 3072], P('dp', None, 'shard'), may hold values from -0.21875 to 0.21875
- frozen_out: bfloat16 [32, 3072, 768], P('dp', 'shard'), may hold values from -0.109375 to 0.109375
- cotangent: bfloat16 [32768, 768], P(('dp', 'shard')), may hold values from -6 to 6
Outputs:
- layer_out: bfloat16 [32768, 768], P(('dp', 'shard'))
- grad_tokens: bfloat16 [32768, 768], P(('dp', 'shard'))
- grad_query: float32 [768, 768], P(('dp', 'shard'))
- grad_key: float32 [768, 768], P(('dp', 'shard'))
- grad_value: float32 [768, 768], P(('dp', 'shard'))
- grad_output: float32 [768, 768], P(('dp', 'shard'))
- grad_ln1_gain: float32 [768], P(('dp', 'shard'))
- grad_ln1_bias: float32 [768], P(('dp', 'shard'))
- grad_ln2_gain: float32 [768], P(('dp', 'shard'))
- grad_ln2_bias: float32 [768], P(('dp', 'shard'))
- grad_gate_new: float32 [768, 32], P(('dp', 'shard'))
- grad_new_in: float32 [32, 768, 3072], P('dp', None, 'shard')
- grad_new_out: float32 [32, 3072, 768], P('dp', 'shard')
Inputs may be any that keep to these rules, and one draw needn't show every extreme that they name: `bounds`: for each group the first boundary is below 256 and the second above 768, so the middle document begins on the group's first device and ends on its last; in one group the boundaries are 0 and 1024. `routes`: each token names two different experts; among the 256 tokens of one device no expert is named more than 16 times, a bound that some block reaches.
All inputs are finite; a program needn't handle non-finite values.
Results may differ from a plain program's by a relative error of at most 0.02.
Values may be sent and summed in bfloat16 or wider, within the bound.
No kernel may reach another device: no remote copies, remote signals or barrier semaphores. Data moves between devices by JAX's collectives and lax.ppermute only.
A program may use at most 192 MiB of HBM per device.

v0:
```python
import math

import jax
import jax.numpy as jnp
from jax import lax
from jax.sharding import PartitionSpec as P

HEAD_DIM = 64


def sent_together(arrays, axis, dim, along):
    widths = [math.prod(a.shape[along:]) for a in arrays]
    both = jnp.concatenate(
        [a.reshape(*a.shape[:along], w) for a, w in zip(arrays, widths)], axis=along
    )
    out = lax.all_gather(both, axis, axis=dim, tiled=True)
    blocks = jnp.split(out, [sum(widths[:k]) for k in range(1, len(widths))], axis=along)
    return tuple((b.reshape(*out.shape[:along], *a.shape[along:]) for a, b in zip(arrays, blocks)))


def in_one_piece(arrays, axis, dim, along):
    widths = [a.shape[along] for a in arrays]
    both = jnp.concatenate(arrays, axis=along)
    out = lax.all_gather(both, axis, axis=dim, tiled=True)
    return tuple(jnp.split(out, [sum(widths[:k]) for k in range(1, len(widths))], axis=along))


def gather_turned(arrays, axis, dims):
    turned = [jnp.moveaxis(a, dim, 0) for a, dim in zip(arrays, dims)]
    both = jnp.concatenate([t.reshape(len(t), -1) for t in turned], axis=1)
    out, at, outs = (lax.all_gather(both, axis, axis=0, tiled=True), 0, [])
    for t, dim in zip(turned, dims):
        share = out[:, at : at + t[0].size].reshape(-1, *t.shape[1:])
        outs.append(jnp.moveaxis(share, 0, dim))
        at += t[0].size
    return tuple(outs)


def side_by_side(arrays, axis, dim, along):
    widths = [a.shape[along] for a in arrays]
    both = jnp.concatenate(arrays, axis=along)
    out = lax.psum_scatter(both, axis, scatter_dimension=dim, tiled=True)
    return tuple(jnp.split(out, [sum(widths[:k]) for k in range(1, len(widths))], axis=along))


def split_up(array, dim, peers):
    before, after = (array.shape[:dim], array.shape[dim + 1 :])
    return jnp.moveaxis(array.reshape(*before, peers, -1, *after), dim, 0)


def sum_together(arrays, axis, dims):
    peers = lax.axis_size(axis)
    blocks = [split_up(a, dim, peers) for a, dim in zip(arrays, dims)]
    lines = jnp.concatenate([b.reshape(peers, -1) for b in blocks], axis=1)
    extent = max(16, -(-lines.shape[1] // 1024) * 8)
    lines = jnp.pad(lines, ((0, 0), (0, extent * 128 - lines.shape[1]))).reshape(-1, 128)
    flat, at, outs = (lax.psum_scatter(lines, axis, tiled=True).reshape(-1), 0, [])
    for b in blocks:
        part = b[0]
        outs.append(flat[at : at + part.size].reshape(part.shape))
        at += part.size
    return tuple(outs)


def norm_stats(values_in):
    center = values_in - jnp.mean(values_in, -1, keepdims=True)
    scaling = lax.rsqrt(jnp.mean(center * center, -1, keepdims=True) + 1e-05)
    return (center * scaling, scaling)


def norm_back(grad_normed, normed, scaling):
    mean_grad = jnp.mean(grad_normed, -1, keepdims=True)
    mean_cross = jnp.mean(grad_normed * normed, -1, keepdims=True)
    return scaling * (grad_normed - mean_grad - normed * mean_cross)


def contract_rows(left, right):
    return lax.dot_general(
        left, right, (((0,), (0,)), ((), ())), preferred_element_type=jnp.float32
    )


def contract_cols(left, right):
    return lax.dot_general(
        left, right, (((1,), (1,)), ((), ())), preferred_element_type=jnp.float32
    )


def expert_forward(rows_in, weight_in, weight_out):
    pre_act = jnp.dot(rows_in, weight_in, preferred_element_type=jnp.float32)
    hidden = jax.nn.gelu(pre_act, approximate=True).astype(jnp.bfloat16)
    return jnp.dot(hidden, weight_out, preferred_element_type=jnp.float32)


def gelu_tanh(values_in):
    return jax.nn.gelu(values_in, approximate=True)


def expert_backward(rows_in, grad_rows, weight_in, weight_out, wanted):
    pre_act = jnp.dot(rows_in, weight_in, preferred_element_type=jnp.float32)
    activ, pull_gelu = jax.vjp(gelu_tanh, pre_act)
    hidden = activ.astype(jnp.bfloat16)
    grad_hidden = contract_cols(grad_rows, weight_out)
    grad_pre = pull_gelu(grad_hidden)[0].astype(jnp.bfloat16)
    grad_input = contract_cols(grad_pre, weight_in)
    if wanted:
        return (grad_input, contract_rows(rows_in, grad_pre), contract_rows(hidden, grad_rows))
    return (grad_input, None, None)


def score_block(query_heads, key_heads, allowed, scaling):
    scores = (
        jnp.einsum("qhd,khd->hqk", query_heads, key_heads, preferred_element_type=jnp.float32)
        * scaling
    )
    return jnp.where(allowed[None], scores, -1e30)


def per_device(
    tokens,
    bounds,
    routes,
    ln1_gain,
    ln1_bias,
    query_weight,
    key_weight,
    value_weight,
    output_weight,
    ln2_gain,
    ln2_bias,
    gate_new,
    gate_frozen,
    new_in,
    new_out,
    frozen_in,
    frozen_out,
    cotangent,
):
    fl32 = jnp.float32
    bf16 = jnp.bfloat16
    tok_rows = tokens.shape[0]
    model_width = tokens.shape[1]
    experts_half = lax.axis_size("dp")
    shard_count = lax.axis_size("shard")
    capacity = 2 * tok_rows // experts_half
    group_len = tok_rows * shard_count
    head_count = model_width // HEAD_DIM
    scaling = HEAD_DIM ** (-0.5)
    gathered = sent_together(
        (
            query_weight,
            key_weight,
            value_weight,
            output_weight,
            ln1_gain,
            ln1_bias,
            ln2_gain,
            ln2_bias,
            gate_new,
            gate_frozen,
        ),
        ("dp", "shard"),
        0,
        1,
    )
    (
        w_query,
        w_key,
        w_value,
        w_output,
        gain_one,
        bias_one,
        gain_two,
        bias_two,
        gate_mine,
        gate_old,
    ) = gathered
    gate_all = jnp.concatenate([gate_mine, gate_old], 1)
    x_in = tokens.astype(fl32)
    normed_one, scale_one = norm_stats(x_in)
    n_one = (normed_one * gain_one.astype(fl32) + bias_one.astype(fl32)).astype(bf16)
    queries = jnp.dot(n_one, w_query, preferred_element_type=fl32).astype(bf16)
    key_local = jnp.dot(n_one, w_key, preferred_element_type=fl32).astype(bf16)
    value_local = jnp.dot(n_one, w_value, preferred_element_type=fl32).astype(bf16)
    keys_all, values_all = in_one_piece((key_local, value_local), "shard", 0, 1)
    offset = lax.axis_index("shard") * tok_rows
    query_pos = offset + jnp.arange(tok_rows, dtype=jnp.int32)
    key_pos = jnp.arange(group_len, dtype=jnp.int32)
    doc_start = bounds[0, 0]
    doc_end = bounds[0, 1]
    query_doc = (query_pos >= doc_start).astype(jnp.int32) + (query_pos >= doc_end).astype(
        jnp.int32
    )
    key_doc = (key_pos >= doc_start).astype(jnp.int32) + (key_pos >= doc_end).astype(jnp.int32)
    allowed = (query_doc[:, None] == key_doc[None, :]) & (key_pos[None, :] <= query_pos[:, None])
    query_heads = queries.reshape(tok_rows, head_count, HEAD_DIM)
    key_heads = keys_all.reshape(group_len, head_count, HEAD_DIM)
    value_heads = values_all.reshape(group_len, head_count, HEAD_DIM)
    scores = score_block(query_heads, key_heads, allowed, scaling)
    highest = jnp.max(scores, -1, keepdims=True)
    exponent = jnp.exp(scores - highest)
    totals = jnp.sum(exponent, -1, keepdims=True)
    attn_prob = exponent / totals
    log_total = highest + jnp.log(totals)
    attended = jnp.einsum(
        "hqk,khd->qhd", attn_prob.astype(bf16), value_heads, preferred_element_type=fl32
    )
    attended = attended.reshape(tok_rows, model_width).astype(bf16)
    resid = x_in + jnp.dot(attended, w_output, preferred_element_type=fl32)
    normed_two, scale_two = norm_stats(resid)
    x_two = (normed_two * gain_two.astype(fl32) + bias_two.astype(fl32)).astype(bf16)
    logits = jnp.dot(x_two, gate_all, preferred_element_type=fl32)
    expert_ids = jnp.arange(2 * experts_half, dtype=jnp.int32)
    pick_zero = routes[:, 0:1] == expert_ids[None, :]
    pick_one = routes[:, 1:2] == expert_ids[None, :]
    logit_zero = jnp.sum(jnp.where(pick_zero, logits, 0.0), -1)
    logit_one = jnp.sum(jnp.where(pick_one, logits, 0.0), -1)
    top_logit = jnp.maximum(logit_zero, logit_one)
    weight_zero = jnp.exp(logit_zero - top_logit)
    weight_one = jnp.exp(logit_one - top_logit)
    comb_zero = weight_zero / (weight_zero + weight_one)
    comb_one = weight_one / (weight_zero + weight_one)
    flat_routes = routes.reshape(-1)
    onehot = (flat_routes[:, None] == expert_ids[None, :]).astype(jnp.int32)
    earlier = jnp.cumsum(onehot, 0) - onehot
    slot_pos = jnp.sum(earlier * onehot, 1).reshape(tok_rows, 2)
    owner = routes % experts_half
    kind = routes // experts_half
    slot_ids = (owner * 2 + kind) * capacity + slot_pos
    slot_range = jnp.arange(4 * tok_rows, dtype=jnp.int32)[:, None]
    place_zero = (slot_range == slot_ids[None, :, 0]).astype(bf16)
    place_one = (slot_range == slot_ids[None, :, 1]).astype(bf16)
    placing = place_zero + place_one
    buffer = jnp.dot(placing, x_two, preferred_element_type=fl32).astype(bf16)
    buffer = buffer.reshape(experts_half, 2 * capacity, model_width)
    received = lax.all_to_all(buffer, "dp", split_axis=0, concat_axis=0, tiled=True)
    full_new_in, full_new_out, full_old_in, full_old_out = gather_turned(
        (new_in[0], new_out[0], frozen_in[0], frozen_out[0]), "shard", (1, 0, 1, 0)
    )
    new_rows = received[:, :capacity].reshape(-1, model_width)
    old_rows = received[:, capacity:].reshape(-1, model_width)
    out_new = expert_forward(new_rows, full_new_in, full_new_out).reshape(-1, capacity, model_width)
    out_old = expert_forward(old_rows, full_old_in, full_old_out).reshape(-1, capacity, model_width)
    expert_result = jnp.concatenate([out_new, out_old], 1).astype(bf16)
    returned = lax.all_to_all(expert_result, "dp", split_axis=0, concat_axis=0, tiled=True).reshape(
        4 * tok_rows, model_width
    )
    out_zero = contract_rows(place_zero, returned)
    out_one = contract_rows(place_one, returned)
    layer_out = (resid + comb_zero[:, None] * out_zero + comb_one[:, None] * out_one).astype(bf16)
    again = sent_together(
        (query_weight, key_weight, value_weight, output_weight, ln1_gain, ln2_gain, gate_new),
        ("dp", "shard"),
        0,
        1,
    )
    back_query, back_key, back_value, back_output, back_gain_one, back_gain_two, back_gate = again
    gate_back = jnp.concatenate([back_gate, gate_old], 1)
    grad_out = cotangent.astype(fl32)
    dcomb_zero = jnp.sum(grad_out * out_zero, -1)
    dcomb_one = jnp.sum(grad_out * out_one, -1)
    mean_dcomb = comb_zero * dcomb_zero + comb_one * dcomb_one
    dlog_zero = comb_zero * (dcomb_zero - mean_dcomb)
    dlog_one = comb_one * (dcomb_one - mean_dcomb)
    dlogits = (
        jnp.where(pick_zero, dlog_zero[:, None], 0.0) + jnp.where(pick_one, dlog_one[:, None], 0.0)
    ).astype(bf16)
    grad_gate_all = contract_rows(x_two, dlogits)
    grad_gate_mine = grad_gate_all[:, :experts_half]
    grad_x_two = contract_cols(dlogits, gate_back)
    grad_y_zero = (comb_zero[:, None] * grad_out).astype(bf16)
    grad_y_one = (comb_one[:, None] * grad_out).astype(bf16)
    grad_buffer = jnp.dot(place_zero, grad_y_zero, preferred_element_type=fl32) + jnp.dot(
        place_one, grad_y_one, preferred_element_type=fl32
    )
    grad_buffer = grad_buffer.astype(bf16).reshape(experts_half, 2 * capacity, model_width)
    grad_received = lax.all_to_all(grad_buffer, "dp", split_axis=0, concat_axis=0, tiled=True)
    grad_new_rows = grad_received[:, :capacity].reshape(-1, model_width)
    grad_old_rows = grad_received[:, capacity:].reshape(-1, model_width)
    input_new, grad_in_new, grad_out_new = expert_backward(
        new_rows, grad_new_rows, full_new_in, full_new_out, True
    )
    input_old, unused_in, unused_out = expert_backward(
        old_rows, grad_old_rows, full_old_in, full_old_out, False
    )
    input_grads = jnp.concatenate(
        [
            input_new.reshape(-1, capacity, model_width),
            input_old.reshape(-1, capacity, model_width),
        ],
        1,
    ).astype(bf16)
    owned_in, owned_out = (
        lax.psum_scatter(
            grad_in_new.astype(jnp.bfloat16), "shard", scatter_dimension=1, tiled=True
        ).astype(jnp.float32),
        lax.psum_scatter(
            grad_out_new.astype(jnp.bfloat16), "shard", scatter_dimension=0, tiled=True
        ).astype(jnp.float32),
    )
    grad_new_in = owned_in[None]
    grad_new_out = owned_out[None]
    grad_back = lax.all_to_all(input_grads, "dp", split_axis=0, concat_axis=0, tiled=True).reshape(
        4 * tok_rows, model_width
    )
    grad_x_two = grad_x_two + contract_rows(placing, grad_back)
    grad_gain_two = jnp.sum(grad_x_two * normed_two, 0)
    grad_bias_two = jnp.sum(grad_x_two, 0)
    grad_resid = grad_out + norm_back(
        grad_x_two * back_gain_two.astype(fl32), normed_two, scale_two
    )
    grad_attn = grad_resid.astype(bf16)
    grad_w_output = contract_rows(attended, grad_attn)
    grad_attended = contract_cols(grad_attn, back_output).astype(bf16)
    grad_heads = grad_attended.reshape(tok_rows, head_count, HEAD_DIM)
    scores = score_block(query_heads, key_heads, allowed, scaling)
    attn_prob = jnp.exp(scores - log_total)
    grad_prob = jnp.einsum("qhd,khd->hqk", grad_heads, value_heads, preferred_element_type=fl32)
    delta = jnp.sum(attn_prob * grad_prob, -1, keepdims=True)
    grad_score = (attn_prob * (grad_prob - delta)).astype(bf16)
    grad_query = (
        (jnp.einsum("hqk,khd->qhd", grad_score, key_heads, preferred_element_type=fl32) * scaling)
        .reshape(tok_rows, model_width)
        .astype(bf16)
    )
    key_part = (
        jnp.einsum("hqk,qhd->khd", grad_score, query_heads, preferred_element_type=fl32) * scaling
    ).reshape(group_len, model_width)
    value_part = jnp.einsum(
        "hqk,qhd->khd", attn_prob.astype(bf16), grad_heads, preferred_element_type=fl32
    ).reshape(group_len, model_width)
    grad_key_sum, grad_value_sum = tuple(
        (
            part.astype(jnp.float32)
            for part in side_by_side(
                (key_part.astype(jnp.bfloat16), value_part.astype(jnp.bfloat16)), "shard", 0, 1
            )
        )
    )
    grad_key = grad_key_sum.astype(bf16)
    grad_value = grad_value_sum.astype(bf16)
    grad_w_query = contract_rows(n_one, grad_query)
    grad_w_key = contract_rows(n_one, grad_key)
    grad_w_value = contract_rows(n_one, grad_value)
    grad_n_one = (
        contract_cols(grad_query, back_query)
        + contract_cols(grad_key, back_key)
        + contract_cols(grad_value, back_value)
    )
    grad_gain_one = jnp.sum(grad_n_one * normed_one, 0)
    grad_bias_one = jnp.sum(grad_n_one, 0)
    grad_tokens = (
        grad_resid + norm_back(grad_n_one * back_gain_one.astype(fl32), normed_one, scale_one)
    ).astype(bf16)
    owned = sum_together(
        (
            grad_w_query,
            grad_w_key,
            grad_w_value,
            grad_w_output,
            grad_gain_one,
            grad_bias_one,
            grad_gain_two,
            grad_bias_two,
            grad_gate_mine,
        ),
        ("dp", "shard"),
        (0, 0, 0, 0, 0, 0, 0, 0, 0),
    )
    return (
        layer_out,
        grad_tokens,
        owned[0],
        owned[1],
        owned[2],
        owned[3],
        owned[4],
        owned[5],
        owned[6],
        owned[7],
        owned[8],
        grad_new_in,
        grad_new_out,
    )


def solution(mesh):
    in_specs = (
        P(("dp", "shard"), None),
        P("dp", None),
        P(("dp", "shard"), None),
        P(("dp", "shard")),
        P(("dp", "shard")),
        P(("dp", "shard"), None),
        P(("dp", "shard"), None),
        P(("dp", "shard"), None),
        P(("dp", "shard"), None),
        P(("dp", "shard")),
        P(("dp", "shard")),
        P(("dp", "shard"), None),
        P(("dp", "shard"), None),
        P("dp", None, "shard"),
        P("dp", "shard", None),
        P("dp", None, "shard"),
        P("dp", "shard", None),
        P(("dp", "shard"), None),
    )
    out_specs = (
        P(("dp", "shard"), None),
        P(("dp", "shard"), None),
        P(("dp", "shard"), None),
        P(("dp", "shard"), None),
        P(("dp", "shard"), None),
        P(("dp", "shard"), None),
        P(("dp", "shard")),
        P(("dp", "shard")),
        P(("dp", "shard")),
        P(("dp", "shard")),
        P(("dp", "shard"), None),
        P("dp", None, "shard"),
        P("dp", "shard", None),
    )
    return jax.shard_map(
        per_device, mesh=mesh, in_specs=in_specs, out_specs=out_specs, check_vma=False
    )
```

profile of v0, /device:TPU:1, one launch (start us, length us, event | category | flops | bytes accessed | tf_op | source)
XLA Modules:
  0.0 1055.9 jit_solution(3767266208362904803)
XLA Ops:
  14.3 202.1 %all-gather.11.cloned.1.call-done = bf16[128,6,3140]{2,1,0:T(8,128)(2,1)} async-done(((bf16[1,6,3140]{2,1,0:T(8,128)(2,1)}), bf16[128,6,3140]{2,1,0:T(8,128)(2,1)}) %all-gather.11.cloned.1.call-update) | async-done | bytes 4823056 | tf_op jit(solution)/shard_map/all_gather | solution.py:16
  216.4 9.9 reshape.410
  235.8 4.3 pad_maximum_fusion
  249.2 16.0 %all-gather.7.cloned.1.call-done = bf16[1024,1536]{1,0:T(8,128)(2,1)} async-done(((bf16[256,1536]{1,0:T(8,128)(2,1)}), bf16[1024,1536]{1,0:T(8,128)(2,1)}) %all-gather.7.cloned.1.call-update) | async-done | bytes 3145744 | tf_op jit(solution)/shard_map/all_gather | solution.py:24
  280.9 3.9 fusion.62
  288.2 32.8 %all_to_all.20 = bf16[32,32,768]{2,1,0:T(8,128)(2,1)S(1)} all-to-all(bf16[32,32,768]{2,1,0:T(8,128)(2,1)S(1)} %bitcast.115), channel_id=1, replica_groups=mesh['dp'=32,'shard'=4] {'dp'}, dimensions={0} | all-to-all | bytes 3145728 | tf_op jit(solution)/shard_map/all_to_all | solution.py:236
  322.2 85.1 %all-gather.9.cloned.1.call-done = bf16[3072,3072]{1,0:T(8,128)(2,1)} async-done(((bf16[768,3072]{1,0:T(8,128)(2,1)}), bf16[3072,3072]{1,0:T(8,128)(2,1)}) %all-gather.9.cloned.1.call-update) | async-done | bytes 18874384 | tf_op jit(solution)/shard_map/all_gather | solution.py:31
  407.3 4.9 fusion.27
  412.2 8.4 fusion.53
  428.5 7.1 all-to-all-start.1
  440.5 16.4 %all-to-all-done.1 = bf16[32,32,768]{2,1,0:T(8,128)(2,1)} async-done(((bf16[32,32,768]{2,1,0:T(8,128)(2,1)}), bf16[32,32,768]{2,1,0:T(8,128)(2,1)}, u32[]{:S(2)}, u32[]{:S(2)}) %all-to-all-start.1) | async-done | bytes 1572896 | tf_op jit(solution)/shard_map/all_to_all | solution.py:245
  465.8 29.4 %all_to_all.21 = bf16[32,32,768]{2,1,0:T(8,128)(2,1)S(1)} all-to-all(bf16[32,32,768]{2,1,0:T(8,128)(2,1)S(1)} %bitcast.106), channel_id=1, replica_groups=mesh['dp'=32,'shard'=4] {'dp'}, dimensions={0} | all-to-all | bytes 3145728 | tf_op jit(solution)/shard_map/all_to_all | solution.py:277
  495.3 7.3 fusion.21
  502.6 9.0 fusion.8
  511.6 4.8 fusion.47
  516.4 9.0 fusion.56
  526.7 5.4 all-to-all-start.3
  532.3 129.6 %all-gather.13.cloned.1.call-done = bf16[128,6,3106]{2,1,0:T(8,128)(2,1)} async-done(((bf16[1,6,3106]{2,1,0:T(8,128)(2,1)}), bf16[128,6,3106]{2,1,0:T(8,128)(2,1)}) %all-gather.13.cloned.1.call-update) | async-done | bytes 4770832 | tf_op jit(solution)/shard_map/all_gather | solution.py:16
  661.9 9.9 reshape.412
  685.7 11.8 %multiply_reduce_fusion = (f32[12,256]{1,0:T(8,128)S(1)}, f32[12,256,1024]{2,1,0:T(8,128)}) fusion(f32[12,256]{1,0:T(8,128)S(1)} %copy-done.20, f32[12,256,1024]{2,1,0:T(8,128)} %copy-done, pred[256,1024]{1,0:T(8,128)(4,1)} %copy-done.3, bf16[256,12,64]{0,2,1:T(8,128)(2,1)S(1)} %bitcast.117, bf16[1024,12,64]{0,2,1:T(8,128)(2,1)} %bitcast.107), kind=kOutput, calls=%fused_computation.1 | convolution fusion | flops 418378752 | bytes 27418624 | tf_op jit(solution)/shard_map/qhd,khd->hqk/dot_general | solution.py:318
  697.4 6.9 fusion.44
  704.3 6.8 multiply_convert_fusion
  715.9 6.2 convolution_convert_fusion.1
  722.4 9.1 convolution_convert_fusion
  732.8 4.9 fusion.61
  749.8 9.8 reduce-scatter.4.cloned.1.call-done
  775.4 12.8 %concatenate.41 = f32[128,18648]{1,0:T(8,128)} concatenate(f32[128,4608]{1,0:T(8,128)} %reshape_reshape.15, f32[128,4608]{1,0:T(8,128)} %reshape_reshape.16, f32[128,4608]{1,0:T(8,128)} %reshape_reshape.17, f32[128,4608]{1,0:T(8,128)} %reshape_reshape.18, f32[128,6]{1,0:T(8,128)S(1)} %reshape.390, f32[128,6]{1,0:T(8,128)S(1)} %reshape.391, f32[128,6]{1,0:T(8,128)S(1)} %reshape.392, ...), dimensions={1} | concatenate | bytes 19095552 | tf_op jit(solution)/shard_map/concatenate | solution.py:54
  788.2 8.5 pad.4
  796.7 10.4 reshape.394
  808.2 8.4 reduce-scatter.6.cloned.1.call-done
  819.4 54.0 %reduce-scatter.8.cloned.1.call-done = bf16[768,768]{1,0:T(8,128)(2,1)} async-done(((bf16[3072,768]{1,0:T(8,128)(2,1)}), bf16[768,768]{1,0:T(8,128)(2,1)}) %reduce-scatter.8.cloned.1.call-update) | async-done | bytes 1179664 | tf_op jit(solution)/shard_map/reduce_scatter | solution.py:297
  876.3 167.1 %all-reduce.4.cloned.1.call-done = f32[19456,128]{1,0:T(8,128)} async-done(((f32[19456,128]{1,0:T(8,128)}), f32[19456,128]{1,0:T(8,128)}) %all-reduce.4.cloned.1.call-update) | async-done | bytes 9961488
  (299 shorter events, 128.6 us)
Async XLA Ops:
  7.2 209.2 %all-gather.11.cloned.1.call-start = ((), (), s32[]{:S(2)}) async-start(), calls=%async_computation.12 | async-start | bytes 6604800 | tf_op jit(solution)/shard_map/all_gather | solution.py:16
  11.7 253.4 %all-gather.7.cloned.1.call-start = ((), (), s32[]{:S(2)}) async-start(), calls=%async_computation.7 | async-start | bytes 3932160 | tf_op jit(solution)/shard_map/all_gather | solution.py:24
  13.0 234.1 %copy-start.27 = (f32[256]{0:T(256)}, f32[256]{0:T(256)S(1)}, u32[]{:S(2)}) copy-start(f32[256]{0:T(256)S(1)} %broadcast_multiply_fusion.5) | copy-start | bytes 3076
  13.0 215.7 %copy-start.2 = (bf16[256,768]{1,0:T(8,128)(2,1)S(1)}, bf16[256,768]{1,0:T(8,128)(2,1)}, u32[]{:S(2)}) copy-start(bf16[256,768]{1,0:T(8,128)(2,1)} %param.18) | copy-start | bytes 1179652
  14.3 232.8 %copy-start.29 = (f32[256]{0:T(256)}, f32[256]{0:T(256)S(1)}, u32[]{:S(2)}) copy-start(f32[256]{0:T(256)S(1)} %add_rsqrt_fusion.1) | copy-start | bytes 3076
  233.3 173.9 %all-gather.9.cloned.1.call-start = ((), (), s32[]{:S(2)}) async-start(), calls=%async_computation.8 | async-start | bytes 23592960 | tf_op jit(solution)/shard_map/all_gather | solution.py:31
  247.1 30.7 %copy-start.3 = (pred[256,1024]{1,0:T(8,128)(4,1)}, pred[256,1024]{1,0:T(8,128)(4,1)S(1)}, u32[]{:S(2)}) copy-start(pred[256,1024]{1,0:T(8,128)(4,1)S(1)} %fusion.77) | copy-start | bytes 786436
  287.0 125.1 %copy-start.37 = (f32[256]{0:T(256)}, f32[256]{0:T(256)S(1)}, u32[]{:S(2)}) copy-start(f32[256]{0:T(256)S(1)} %broadcast_multiply_fusion.4) | copy-start | bytes 3076
  287.3 124.9 %copy-start.52 = (f32[256]{0:T(256)}, f32[256]{0:T(256)S(1)}, u32[]{:S(2)}) copy-start(f32[256]{0:T(256)S(1)} %add_rsqrt_fusion) | copy-start | bytes 3076
  287.5 150.4 %copy-start.9 = (bf16[256,768]{1,0:T(8,128)(2,1)}, bf16[256,768]{1,0:T(8,128)(2,1)S(1)}, u32[]{:S(2)}) copy-start(bf16[256,768]{1,0:T(8,128)(2,1)S(1)} %add_convert_fusion.2) | copy-start | bytes 1179652
  427.2 31.8 %copy-start.5 = (bf16[256,768]{1,0:T(8,128)(2,1)S(1)}, bf16[256,768]{1,0:T(8,128)(2,1)}, u32[]{:S(2)}) copy-start(bf16[256,768]{1,0:T(8,128)(2,1)} %param.35) | copy-start | bytes 1179652
  428.5 28.3 %all-to-all-start.1 = ((bf16[32,32,768]{2,1,0:T(8,128)(2,1)}), bf16[32,32,768]{2,1,0:T(8,128)(2,1)}, u32[]{:S(2)}, u32[]{:S(2)}) async-start(bf16[32,32,768]{2,1,0:T(8,128)(2,1)} %pad_maximum_fusion.2), calls=%async_computation.1 | async-start | bytes 3145728 | tf_op jit(solution)/shard_map/all_to_all | solution.py:245
  435.6 226.3 %all-gather.13.cloned.1.call-start = ((), (), s32[]{:S(2)}) async-start(), calls=%async_computation.13 | async-start | bytes 6604800 | tf_op jit(solution)/shard_map/all_gather | solution.py:16
  440.5 24.5 %copy-start.63 = (s32[256]{0:T(256)S(1)}, s32[256]{0:T(256)}, u32[]{:S(2)}) copy-start(s32[256]{0:T(256)} %get-tuple-element.30) | copy-start | bytes 3076
  463.6 39.0 %slice-start.13 = ((s8[6291456]{0:T(1024)(128)(4,1)}), s8[4194304]{0:T(1024)(128)(4,1)S(1)}, s32[]{:S(2)}) async-start(s8[6291456]{0:T(1024)(128)(4,1)} %bitcast.149), calls=%async_computation.28 | async-start | bytes 8388608
  526.7 151.1 %all-to-all-start.3 = ((bf16[32,32,768]{2,1,0:T(8,128)(2,1)}), bf16[32,32,768]{2,1,0:T(8,128)(2,1)}, u32[]{:S(2)}, u32[]{:S(2)}) async-start(bf16[32,32,768]{2,1,0:T(8,128)(2,1)} %pad_maximum_fusion.3), calls=%async_computation.3 | async-start | bytes 3145728 | tf_op jit(solution)/shard_map/all_to_all | solution.py:303
  532.2 143.6 %copy-start.26 = (f32[12,256]{1,0:T(8,128)S(1)}, f32[12,256]{1,0:T(8,128)}, u32[]{:S(2)}) copy-start(f32[12,256]{1,0:T(8,128)} %copy-done.25) | copy-start | bytes 36868
  532.2 144.2 %copy-start.40 = (f32[256]{0:T(256)S(1)}, f32[256]{0:T(256)}, u32[]{:S(2)}) copy-start(f32[256]{0:T(256)} %copy-done.39) | copy-start | bytes 3076
  532.2 144.2 %copy-start.42 = (f32[256]{0:T(256)S(1)}, f32[256]{0:T(256)}, u32[]{:S(2)}) copy-start(f32[256]{0:T(256)} %copy-done.41) | copy-start | bytes 3076
  532.2 144.2 %copy-start.59 = (f32[256]{0:T(256)S(1)}, f32[256]{0:T(256)}, u32[]{:S(2)}) copy-start(f32[256]{0:T(256)} %copy-done.58) | copy-start | bytes 3076
  532.2 144.2 %copy-start.61 = (f32[256]{0:T(256)S(1)}, f32[256]{0:T(256)}, u32[]{:S(2)}) copy-start(f32[256]{0:T(256)} %copy-done.60) | copy-start | bytes 3076
  532.2 144.2 %copy-start.44 = (s32[256,1]{0,1:T(1,128)S(1)}, s32[256,1]{0,1:T(1,128)}, u32[]{:S(2)}) copy-start(s32[256,1]{0,1:T(1,128)} %copy-done.43) | copy-start | bytes 3076
  532.2 144.2 %copy-start.47 = (s32[256,1]{0,1:T(1,128)S(1)}, s32[256,1]{0,1:T(1,128)}, u32[]{:S(2)}) copy-start(s32[256,1]{0,1:T(1,128)} %copy-done.46) | copy-start | bytes 3076
  532.2 144.2 %copy-start.54 = (f32[256]{0:T(256)S(1)}, f32[256]{0:T(256)}, u32[]{:S(2)}) copy-start(f32[256]{0:T(256)} %get-tuple-element.33) | copy-start | bytes 3076
  532.3 145.5 %copy-start.38 = (f32[256]{0:T(256)S(1)}, f32[256]{0:T(256)}, u32[]{:S(2)}) copy-start(f32[256]{0:T(256)} %copy-done.37) | copy-start | bytes 3076
  532.3 145.5 %copy-start.51 = (s32[256]{0:T(256)S(1)}, s32[256]{0:T(256)}, u32[]{:S(2)}) copy-start(s32[256]{0:T(256)} %get-tuple-element.29) | copy-start | bytes 3076
  532.3 145.5 %copy-start.53 = (f32[256]{0:T(256)S(1)}, f32[256]{0:T(256)}, u32[]{:S(2)}) copy-start(f32[256]{0:T(256)} %copy-done.52) | copy-start | bytes 3076
  532.3 145.5 %copy-start.64 = (s32[256]{0:T(256)S(1)}, s32[256]{0:T(256)}, u32[]{:S(2)}) copy-start(s32[256]{0:T(256)} %get-tuple-element.30) | copy-start | bytes 3076
  532.3 227.3 %reduce-scatter.4.cloned.1.call-start = ((), (), s32[]{:S(2)}) async-start(), calls=%async_computation.9 | async-start | bytes 3932160 | tf_op jit(solution)/shard_map/reduce_scatter | solution.py:42
  715.9 100.7 %reduce-scatter.6.cloned.1.call-start = ((), (), s32[]{:S(2)}) async-start(), calls=%async_computation.10 | async-start | bytes 5898240 | tf_op jit(solution)/shard_map/reduce_scatter | solution.py:294
  722.2 151.3 %reduce-scatter.8.cloned.1.call-start = ((), (), s32[]{:S(2)}) async-start(), calls=%async_computation.11 | async-start | bytes 5898240 | tf_op jit(solution)/shard_map/reduce_scatter | solution.py:297
  731.5 311.8 %all-reduce.4.cloned.1.call-start = ((), (), s32[]{:S(2)}) async-start(), calls=%async_computation.14 | async-start | bytes 19922944
  (64 other events, 510.3 us)
Sparse Core Ops, SparseCore 0:
  11.9 204.4 all-gather.10
  233.4 31.7 all-gather.6
  266.9 140.3 all-gather.8
  438.4 223.4 all-gather.12
  716.0 43.5 reduce-scatter.3
  762.3 54.2 reduce-scatter.5
  819.2 54.1 reduce-scatter.7
  879.3 163.9 all-reduce.3
where the time goes:
time: 1060 us
  waiting for transfers between devices  689 us (65%)
  matrix products  135 us (13%)
  local copies, waits for them, and re-layouts  97.3 us (9%)
  blocking collectives  62.1 us (6%)
  other arithmetic  43.6 us (4%)
  between operations  15.7 us (1%)
  starting transfers between devices  13.2 us (1%)
    all_gather x2, waiting for transfers between devices, sent_together(): out = lax.all_gather(both, axis, axis=dim, tiled=True)  332 us
    unnamed x9, waiting for transfers between devices  167 us
    all_gather x1, waiting for transfers between devices, gather_turned(): out, at, outs = (lax.all_gather(both, axis, axis=0, tiled=True), 0, [])  85.1 us
    reduce_scatter x1, waiting for transfers between devices, per_device(): lax.psum_scatter(grad_out_new.astype(jnp.bfloat16), 'shard', scatter_dime...  54 us
    dot_general x9, matrix products, contract_cols(): lax.dot_general(left, right, (((1,), (1,)), ((), ())), preferred_element_...  39.1 us
    dot_general x9, matrix products, contract_rows(): lax.dot_general(left, right, (((0,), (0,)), ((), ())), preferred_element_...  32.9 us
    all_to_all x1, blocking collectives, per_device(): lax.all_to_all(buffer, 'dp', split_axis=0, concat_axis=0, tiled=True)  32.8 us
    all_to_all x1, blocking collectives, per_device(): lax.all_to_all(grad_buffer, 'dp', split_axis=0, concat_axis=0, tiled=True)  29.4 us
  transfers between devices with their start and end apart: 10, of which 9 were waited for; matrix products, arithmetic and copies ran while one was open for 18% of the time, Pallas kernels for 0%

commit v1 on v0

v1 whole, which is shorter than its diff:
```python
import functools

import jax
import jax.numpy as jnp
from jax import lax
from jax.experimental import pallas as pl
from jax.experimental.pallas import tpu as pltpu
from jax.sharding import PartitionSpec as P

HEAD_DIM = 64
BOTH = ("dp", "shard")
F32 = jnp.float32
BF16 = jnp.bfloat16
I32 = jnp.int32
VMEM_BYTES = 56 * 2**20
PAD = 8
SMEM = pltpu.SMEM
VMEM = pltpu.VMEM


def mul(left, right):
    return jnp.dot(left, right, preferred_element_type=F32)


def contract_rows(left, right):
    return lax.dot_general(left, right, (((0,), (0,)), ((), ())), preferred_element_type=F32)


def contract_cols(left, right):
    return lax.dot_general(left, right, (((1,), (1,)), ((), ())), preferred_element_type=F32)


def iota(shape, dim):
    return lax.broadcasted_iota(I32, shape, dim)


def norm_stats(values_in):
    center = values_in - jnp.mean(values_in, -1, keepdims=True)
    scaling = lax.rsqrt(jnp.mean(center * center, -1, keepdims=True) + 1e-05)
    return (center * scaling, scaling)


def norm_back(grad_normed, normed, scaling):
    mean_grad = jnp.mean(grad_normed, -1, keepdims=True)
    mean_cross = jnp.mean(grad_normed * normed, -1, keepdims=True)
    return scaling * (grad_normed - mean_grad - normed * mean_cross)


def in_three(values_in):
    first = values_in.astype(BF16).astype(F32)
    rest = values_in - first
    second = rest.astype(BF16).astype(F32)
    return first, second, rest - second


def in_lanes(terms, rows):
    lane = iota((rows, 128), 1)
    out = jnp.zeros((rows, 128), F32)
    for k, term in enumerate(terms):
        out = jnp.where(lane == k, term, out)
    return out


def spread(held, width, rows_first):
    padded = width // held * PAD
    shape, row_dim = ((width, padded), 0) if rows_first else ((padded, width), 1)
    row, col = iota(shape, row_dim), iota(shape, 1 - row_dim)
    block = block_of(row, held)
    return (col == block * PAD + (row - block * held)).astype(F32).astype(BF16)


def block_of(row, held):
    step = -(-(1 << 16) // held)
    return lax.shift_right_logical(row * step, 16)


def vector_rows(lanes, held, width, which, first=0):
    row = iota((lanes.shape[1], width), 1)
    lane = iota((lanes.shape[1], width), 0) - first
    pick = (lane == row - block_of(row, held) * held).astype(F32)
    wide = mul(lanes, pick.astype(BF16))
    col = iota(wide.shape, 1)
    wanted = iota(wide.shape, 0) == block_of(col, held) * PAD + which
    return jnp.sum(jnp.where(wanted, wide, 0.0), 0, keepdims=True)


def call(body, out_shapes, args, **more):
    return pl.pallas_call(
        body,
        out_shape=out_shapes,
        compiler_params=pltpu.CompilerParams(vmem_limit_bytes=VMEM_BYTES),
        cost_estimate=pl.CostEstimate(flops=1, bytes_accessed=1, transcendentals=1),
        **more,
    )(*args)


tie = lax.optimization_barrier


def shaped(shape, dtype):
    return jax.ShapeDtypeStruct(shape, dtype)


def pack_body(part, in_wide, query_ref, key_ref, value_ref, out_ref, new_ref, old_ref, *refs):
    (gain_one, bias_one, gain_two, bias_two), blocks_ref, work_ref = refs[:4], refs[4], refs[5]
    held, width = out_ref.shape
    half, gates, at = width // 2, new_ref.shape[1], 3 * part
    work_ref[...] = jnp.zeros_like(work_ref)
    for k in range(work_ref.shape[0]):
        for m, ref in enumerate((query_ref, key_ref, value_ref)):
            piece = ref[:, k * part : (k + 1) * part]
            work_ref[k, :held, m * part : (m + 1) * part] = piece.astype(F32)
        work_ref[k, :held, at : at + gates] = new_ref[...].astype(F32)
        work_ref[k, :held, at + gates : at + 2 * gates] = old_ref[...].astype(F32)
        side = out_ref[:, k % 2 * half : (k % 2 + 1) * half]
        work_ref[k, :held, in_wide : in_wide + half] = side.astype(F32)
        work_ref[k, held : held + 1, :held] = gain_one[...].astype(F32)
        work_ref[k, held + 1 : held + 2, :held] = bias_one[...].astype(F32)
        work_ref[k, held : held + 1, at : at + held] = gain_two[...].astype(F32)
        work_ref[k, held + 1 : held + 2, at : at + held] = bias_two[...].astype(F32)
    blocks = work_ref[...].astype(BF16)

    def put(k, carry):
        blocks_ref[k] = blocks
        return carry

    lax.fori_loop(0, blocks_ref.shape[0], put, 0)


def slots_body(n_dp, capacity, routes_ref, routes_t_ref, cols_ref, lines_ref):
    rows = routes_ref.shape[0]
    routes = routes_ref[...]
    hot = [
        (iota((rows, 2 * n_dp), 1) == routes[:, k : k + 1]).astype(F32) for k in range(2)
    ]
    earlier = (iota((rows, rows), 1) < iota((rows, rows), 0)).astype(F32).astype(BF16)
    count = mul(earlier, (hot[0] + hot[1]).astype(BF16))
    expert = routes
    base = jnp.where(expert < n_dp, 2 * expert, 2 * expert - 2 * n_dp + 1) * capacity
    cols = [
        base[:, k : k + 1] + jnp.sum(count * hot[k], 1, keepdims=True).astype(I32)
        for k in range(2)
    ]
    lane = iota(cols_ref.shape, 1)
    cols_ref[...] = jnp.where(lane == 0, cols[0], cols[1])
    routes_t = routes_t_ref[...]
    hot_t = [
        (iota((2 * n_dp, rows), 0) == routes_t[k : k + 1]).astype(F32) for k in range(2)
    ]
    later = (iota((rows, rows), 0) < iota((rows, rows), 1)).astype(F32).astype(BF16)
    count_t = mul((hot_t[0] + hot_t[1]).astype(BF16), later)
    base_t = jnp.where(routes_t < n_dp, 2 * routes_t, 2 * routes_t - 2 * n_dp + 1) * capacity
    lines = [
        base_t[k : k + 1] + jnp.sum(count_t * hot_t[k], 0, keepdims=True).astype(I32)
        for k in range(2)
    ]
    sub = iota(lines_ref.shape, 0)
    lines_ref[...] = jnp.where(sub == 0, lines[0], lines[1])


def seen_bias(bounds_ref, first, rows, keys, turned=False):
    query = iota((1, rows) if turned else (rows, 1), int(turned)) + first
    key = iota((keys, 1) if turned else (1, keys), 1 - int(turned))
    start, end = bounds_ref[0, 0], bounds_ref[0, 1]

    def doc(pos):
        return (pos >= start).astype(I32) + (pos >= end).astype(I32)

    seen = (doc(query) == doc(key)) & (key <= query)
    return jnp.where(seen, 0.0, -1e30)


def attention_body(held, bounds_ref, shard_ref, got_ref, *refs):
    x_refs, (weight_ref, vector_ref, n_ref, qkv_ref), refs = refs[:4], refs[4:8], refs[8:]
    near_ref, sib_ref, far_ref, att_wide_ref, total_ref = refs
    tile, width = x_refs[0].shape
    part = att_wide_ref.shape[1]
    shard = shard_ref[0, 0]
    got = got_ref[...]
    weight_ref[...] = mul(spread(held, width, True), got).astype(BF16)
    lanes, last = got[:, :128], got[:, got.shape[1] - 128 :]
    first = 3 * part - (got.shape[1] - 128)
    gain = vector_rows(lanes, held, width, held)
    bias = vector_rows(lanes, held, width, held + 1)
    sub = iota(vector_ref.shape, 0)
    vectors = jnp.where(sub == 0, gain, bias)
    vectors = jnp.where(sub == 2, vector_rows(last, held, width, held, first), vectors)
    vector_ref[...] = jnp.where(
        sub == 3, vector_rows(last, held, width, held + 1, first), vectors
    )
    for k, x_ref in enumerate(x_refs):
        at = pl.ds(pl.multiple_of((shard ^ k) * tile, tile), tile)
        normed, unused = norm_stats(x_ref[...].astype(F32))
        n_one = (normed * gain + bias).astype(BF16)
        n_ref[at, :] = n_one
        out = mul(n_one, weight_ref[...])
        scale = jnp.where(iota(out.shape, 1) < part, HEAD_DIM ** (-0.5), 1.0)
        qkv_ref[at, :] = (out.astype(BF16).astype(F32) * scale).astype(BF16)
    for block in range(4):
        first, keys = block * tile, (block + 1) * tile
        hidden = seen_bias(bounds_ref, first, tile, keys)
        totals = []
        for head in range(part // HEAD_DIM):
            at = head * HEAD_DIM
            query = qkv_ref[first:keys, at : at + HEAD_DIM]
            key = qkv_ref[0:keys, part + at : part + at + HEAD_DIM]
            value = qkv_ref[0:keys, 2 * part + at : 2 * part + at + HEAD_DIM]
            scores = contract_cols(query, key) + hidden
            highest = jnp.max(scores, 1, keepdims=True)
            exponent = jnp.exp(scores - highest)
            total = jnp.sum(exponent, 1, keepdims=True)
            prob = (exponent * (1.0 / total)).astype(BF16)
            att_wide_ref[first:keys, at : at + HEAD_DIM] = mul(prob, value)
            totals.append(highest + jnp.log(total))
        total_ref[:, first:keys] = in_lanes(totals, tile).T[: total_ref.shape[0]]
    for k, put in enumerate((near_ref, sib_ref, far_ref.at[:tile], far_ref.at[tile:])):
        at = pl.ds(pl.multiple_of((shard ^ k) * tile, tile), tile)
        put[...] = att_wide_ref[at, :].astype(BF16)


def router_body(
    held,
    n_dp,
    shard_ref,
    x_ref,
    grad_ref,
    near_ref,
    sib_ref,
    far_ref,
    last_ref,
    mine_ref,
    other_ref,
    gates_ref,
    vector_ref,
    routes_ref,
    lines_ref,
    weight_ref,
    resid_ref,
    x_two_ref,
    comb_ref,
    out_ref,
):
    rows, width = x_ref.shape
    slots = out_ref.shape[0]
    part = near_ref.shape[1]
    shard = shard_ref[0, 0]
    first_core = shard % 2 == 0
    left = jnp.where(first_core, mine_ref[...], other_ref[...])
    right = jnp.where(first_core, other_ref[...], mine_ref[...])
    got = jnp.concatenate([left, right], 1)
    weight_ref[...] = mul(spread(held, width, True), got).astype(BF16)
    gain, bias = vector_ref[2:3, :], vector_ref[3:4, :]
    resid = x_ref[...].astype(F32)
    for k, ref in enumerate((near_ref, sib_ref, far_ref.at[:rows], last_ref.at[rows:])):
        at = pl.ds(pl.multiple_of((shard ^ k) * part, part), part)
        resid = resid + mul(ref[...], weight_ref[at, :])
    resid_ref[...] = resid
    normed, unused = norm_stats(resid)
    x_two = (normed * gain + bias).astype(BF16)
    x_two_ref[...] = x_two
    logits = mul(x_two, gates_ref[:, gates_ref.shape[1] - 128 :])
    lane = iota(logits.shape, 1) - (128 - 2 * n_dp)
    chosen = [
        jnp.sum(jnp.where(lane == routes_ref[:, k : k + 1], logits, 0.0), 1, keepdims=True)
        for k in range(2)
    ]
    top = jnp.maximum(chosen[0], chosen[1])
    raw = [jnp.exp(c - top) for c in chosen]
    comb = [r / (raw[0] + raw[1]) for r in raw]
    comb_ref[...] = in_lanes(comb, rows)
    slot = iota((slots, rows), 0)
    place = [(slot == lines_ref[k : k + 1, :]).astype(F32).astype(BF16) for k in range(2)]
    both = (place[0].astype(F32) + place[1].astype(F32)).astype(BF16)
    out_ref[:, :width] = mul(both, x_two).astype(BF16)
    terms = [in_lanes(in_three(c), rows).astype(BF16) for c in comb]
    placed = mul(place[0], terms[0]) + mul(place[1], terms[1])
    out_ref[:, width : width + 128] = placed.astype(BF16)
    out_ref[:, width + 128 :] = mul(both, grad_ref[...]).astype(BF16)


def expert_body(
    shard_ref,
    rows_ref,
    *refs,
):
    own_refs, sib_refs, far_ref = refs[:2], refs[2:4], refs[4]
    back_ref, grad_y_ref, hidden_ref, grad_pre_ref = refs[5:9]
    held_ref, hid_ref, pre_ref, sum_out_ref, sum_back_ref, sems, out_sems = refs[9:]
    slots, width = grad_y_ref.shape
    wide = width + 128
    chunk = 256
    pieces = [slice(k * chunk, (k + 1) * chunk) for k in range(width // chunk)]
    shard = shard_ref[0, 0]
    sources = (
        own_refs,
        [far_ref.at[shard ^ 2, k] for k in range(2)],
        sib_refs,
        [far_ref.at[shard ^ 3, k] for k in range(2)],
    )
    copies = [
        [
            pltpu.make_async_copy(ref, held_ref.at[k, m], sems.at[k, m])
            for m, ref in enumerate(parts)
        ]
        for k, parts in enumerate(sources)
    ]
    for copy in sum(copies, []):
        copy.start()
    comb = jnp.sum(rows_ref[:, width:wide].astype(F32), 1, keepdims=True)
    grad_y_ref[...] = (comb * rows_ref[:, wide:].astype(F32)).astype(BF16)

    def hide(q, at):
        pre = mul(rows_ref[:, :width], held_ref[q, 0, :, at])
        grad_hidden = contract_cols(grad_y_ref[...], held_ref[q, 1, at, :])
        square = pre * pre
        tanh = jnp.tanh(pre * (0.7978845608028654 + 0.035677408136300125 * square))
        share = 0.5 + 0.5 * tanh
        hid = pre * share
        hid_ref[q, :, at] = hid.astype(BF16)
        slope = share + (hid * (1.0 - share)) * (
            1.5957691216057308 + 0.21406444881780074 * square
        )
        pre_ref[q, :, at] = (grad_hidden * slope).astype(BF16)

    def join(q, at):
        out = mul(hid_ref[q], held_ref[q, 1, :, at])
        back = contract_cols(pre_ref[q], held_ref[q, 0, at, :])
        return out, back

    def saves(q):
        at = pl.ds(pl.multiple_of(q * width, width), width)
        return (
            pltpu.make_async_copy(hid_ref.at[q], hidden_ref.at[:, at], out_sems.at[0, q]),
            pltpu.make_async_copy(pre_ref.at[q], grad_pre_ref.at[:, at], out_sems.at[1, q]),
        )

    for copy in copies[0]:
        copy.wait()
    for at in pieces:
        hide(0, at)
    for k, group in enumerate(copies[1:]):
        for copy in group:
            copy.wait()
        for save in saves(k):
            save.start()
        for at in pieces:
            hide(k + 1, at)
            out, back = join(k, at)
            if k == 0:
                sum_out_ref[:, at] = out
                sum_back_ref[:, at] = back
            else:
                sum_out_ref[:, at] += out
                sum_back_ref[:, at] += back
    last = len(copies) - 1
    for save in saves(last):
        save.start()
    dcomb = jnp.zeros((slots, 1), F32)
    for at in pieces:
        out, back = join(last, at)
        out = (sum_out_ref[:, at] + out).astype(BF16)
        back_ref[:, at] = (sum_back_ref[:, at] + back).astype(BF16)
        last_at = slice(wide + at.start, wide + at.stop)
        back_ref[:, last_at] = out
        dcomb += jnp.sum(rows_ref[:, last_at].astype(F32) * out.astype(F32), 1, keepdims=True)
    back_ref[:, width:wide] = in_lanes(in_three(dcomb), slots).astype(BF16)
    for k in range(len(copies)):
        for save in saves(k):
            save.wait()


def expert_call(shard, rows, weights):
    slots = rows.shape[0]
    width = quarter = weights[0].shape[1]
    inside = pl.BlockSpec(memory_space=VMEM)
    anywhere = pl.BlockSpec(memory_space=pl.ANY)
    return call(
        expert_body,
        (
            shaped(rows.shape, BF16),
            shaped((slots, width), BF16),
            shaped((slots, 4 * quarter), BF16),
            shaped((slots, 4 * quarter), BF16),
        ),
        (shard, rows, *weights),
        in_specs=[pl.BlockSpec(memory_space=SMEM), inside] + [anywhere] * len(weights),
        out_specs=[inside] * 2 + [anywhere] * 2,
        scratch_shapes=[
            pltpu.VMEM((4, 2, quarter, quarter), BF16),
            pltpu.VMEM((4, slots, quarter), BF16),
            pltpu.VMEM((4, slots, quarter), BF16),
            pltpu.VMEM((slots, width), F32),
            pltpu.VMEM((slots, width), F32),
            pltpu.SemaphoreType.DMA((4, 2)),
            pltpu.SemaphoreType.DMA((2, 4)),
        ],
    )


def turn_body(rows_ref, grad_y_ref, rows_t_ref, grad_y_t_ref):
    rows_t_ref[...] = rows_ref[:, : rows_t_ref.shape[0]].T
    grad_y_t_ref[...] = grad_y_ref[...].T


def weight_grad_body(rows_t_ref, grad_y_t_ref, hidden_ref, grad_pre_ref, *refs):
    grads = [
        mul(rows_t_ref[...], grad_pre_ref[...]),
        mul(grad_y_t_ref[...], hidden_ref[...]),
    ]
    for k, ref in enumerate(refs[-2:]):
        grad = grads[k] if len(refs) == 2 else grads[k] + refs[k][...].astype(F32)
        ref[...] = grad.astype(ref.dtype)


def weight_grads(rows_t, grad_y_t, hidden, grad_pre, which, dtype, sibs=()):
    width, slots = grad_y_t.shape
    quarter = hidden.shape[1] // 4
    chunk = 256
    pieces = quarter // chunk
    whole = pl.BlockSpec((width, slots), lambda c: (0, 0))
    piece = pl.BlockSpec((slots, chunk), lambda c: (0, which * pieces + c))
    return call(
        weight_grad_body,
        (shaped((width, quarter), dtype),) * 2,
        (rows_t, grad_y_t, hidden, grad_pre, *sibs),
        grid=(pieces,),
        in_specs=[whole] * 2
        + [piece] * 2
        + [pl.BlockSpec((width, chunk), lambda c: (0, c))] * len(sibs),
        out_specs=[pl.BlockSpec((width, chunk), lambda c: (0, c))] * 2,
    )


def new_grads_body(shard_ref, in_ref, out_ref, far_in_ref, far_out_ref, grad_in_ref, grad_out_ref):
    new_here = shard_ref[0, 0] < 2
    grad_in_ref[0] = jnp.where(new_here, in_ref[...], far_in_ref[0].astype(F32))
    grad_out_ref[0] = jnp.where(new_here, out_ref[...], far_out_ref[0].astype(F32)).T


def new_grads_call(shard, own, far_in, far_out):
    quarter = own[0].shape[0]
    tile = quarter // 3
    piece = pl.BlockSpec((quarter, tile), lambda c: (0, c))
    one = pl.BlockSpec((1, quarter, tile), lambda c: (0, 0, c))
    return call(
        new_grads_body,
        (shaped((1, quarter, quarter), F32),) * 2,
        (shard, *own, far_in, far_out),
        grid=(3,),
        in_specs=[pl.BlockSpec(memory_space=SMEM), piece, piece, one, one],
        out_specs=[one, pl.BlockSpec((1, tile, quarter), lambda c: (0, c, 0))],
    )


def token_back_body(
    held,
    n_dp,
    back_ref,
    cols_ref,
    routes_ref,
    comb_ref,
    grad_ref,
    resid_ref,
    x_two_ref,
    gates_ref,
    vector_ref,
    resid_grad_ref,
    att_ref,
    gate_ref,
):
    rows, width = grad_ref.shape
    slots = back_ref.shape[0]
    slot = iota((rows, slots), 1)
    back = [
        mul(
            (slot == cols_ref[:, k : k + 1]).astype(F32).astype(BF16),
            back_ref[:, : width + 128],
        )
        for k in range(2)
    ]
    dcomb = [jnp.sum(b[:, width:], 1, keepdims=True) for b in back]
    comb = [comb_ref[:, k : k + 1] for k in range(2)]
    mean = comb[0] * dcomb[0] + comb[1] * dcomb[1]
    dlog = [c * (d - mean) for c, d in zip(comb, dcomb)]
    lane = iota((rows, 128), 1) - (128 - 2 * n_dp)
    dlogits = jnp.where(lane == routes_ref[:, 0:1], dlog[0], 0.0)
    dlogits = jnp.where(lane == routes_ref[:, 1:2], dlog[1], dlogits).astype(BF16)
    gate = gates_ref[:, gates_ref.shape[1] - 128 :]
    grad_x_two = contract_cols(dlogits, gate) + back[0][:, :width] + back[1][:, :width]
    normed, scaling = norm_stats(resid_ref[...])
    sums = [jnp.sum(grad_x_two * normed, 0, keepdims=True), jnp.sum(grad_x_two, 0, keepdims=True)]
    gain = vector_ref[2:3, :]
    grad_resid = grad_ref[...].astype(F32) + norm_back(grad_x_two * gain, normed, scaling)
    resid_grad_ref[...] = grad_resid
    att_ref[...] = grad_resid.astype(BF16)
    spread_all = spread(held, width, False)
    turned = contract_cols(spread_all, x_two_ref[...]).astype(BF16)
    own_gates = jnp.where(lane < n_dp, dlogits.astype(F32), 0.0).astype(BF16)
    last = 128 - 2 * n_dp + n_dp
    gate_ref[...] = mul(turned, own_gates) + sums_in_lanes(spread_all, sums, last)


def sums_in_lanes(spread_all, sums, first):
    sub = iota((128, sums[0].shape[1]), 0)
    lines = jnp.zeros(sub.shape, F32)
    for k, row in enumerate(sums):
        high, low, unused = in_three(row)
        lines = jnp.where(sub == first + 2 * k, high, lines)
        lines = jnp.where(sub == first + 2 * k + 1, low, lines)
    return contract_cols(spread_all, lines.astype(BF16))


def projection_back_body(
    held,
    shard_ref,
    att_ref,
    weight_ref,
    near_ref,
    sib_ref,
    far_ref,
    far_sib_ref,
    grad_ref,
    *refs,
):
    out_refs, all_ref, owned_ref = refs[:4], *refs[4:]
    tile, width = near_ref.shape
    part = att_ref.shape[1]
    shard = shard_ref[0, 0]
    for k, ref in enumerate((near_ref, sib_ref, far_ref, far_sib_ref)):
        at = pl.ds(pl.multiple_of((shard ^ k) * tile, tile), tile)
        all_ref[at, :] = ref[...]
    mine = pl.ds(pl.multiple_of(shard * part, part), part)
    grad_ref[...] = contract_cols(all_ref[...], weight_ref[mine, :]).astype(BF16)
    turned = contract_cols(spread(held, part, False), att_ref[...].astype(BF16)).astype(BF16)
    owned = mul(turned, all_ref[...]).astype(BF16)
    extent = owned.shape[0]
    for k in range(width // part):
        owned_ref[k * extent : (k + 1) * extent, :] = owned[:, k * part : (k + 1) * part]
    for k, out_ref in enumerate(out_refs):
        at = pl.ds(pl.multiple_of((shard ^ k) * extent, extent), extent)
        out_ref[...] = owned_ref[at, :]


def assemble_body(shard_ref, all_ref, near_ref, sib_ref, far_ref, last_ref, out_ref):
    rows, part = near_ref.shape
    shard = shard_ref[0, 0]
    step = pl.program_id(0)
    for k, ref in enumerate((near_ref, sib_ref, far_ref, last_ref)):
        at = pl.ds(pl.multiple_of((shard ^ k) * rows, rows), rows)

        @pl.when(step == 0)
        def _(at=at, ref=ref):
            out_ref[at, :] = ref[:, :128]

        @pl.when(step == 1)
        def _(at=at, ref=ref):
            out_ref[at, : part - 128] = ref[:, 128:]
            out_ref[at, part - 128 :] = jnp.zeros((rows, 256 - part), BF16)


def attention_back_body(
    held,
    bounds_ref,
    shard_ref,
    n_ref,
    qkv_ref,
    att_ref,
    total_ref,
    weight_ref,
    gate_ref,
    grad_ref,
    *refs,
):
    x_refs, owned_ref, part_refs = refs[:4], refs[4], refs[5:9]
    grads_ref, key_ref, value_ref = refs[9:]
    tile, width = x_refs[0].shape
    part = att_ref.shape[1]
    shard = shard_ref[0, 0]
    key_ref[...] = jnp.zeros_like(key_ref)
    value_ref[...] = jnp.zeros_like(value_ref)
    heads = part // HEAD_DIM
    for block in range(4):
        first, keys = block * tile, (block + 1) * tile
        hidden = seen_bias(bounds_ref, first, tile, keys, True)
        product = grad_ref[first:keys, :].astype(F32) * att_ref[first:keys, :]
        deltas = [
            jnp.sum(product[:, k * HEAD_DIM : (k + 1) * HEAD_DIM], 1, keepdims=True)
            for k in range(heads)
        ]
        deltas = in_lanes(deltas, tile).T
        queries = []
        for head in range(heads):
            at = head * HEAD_DIM
            mine = slice(at, at + HEAD_DIM)
            query = qkv_ref[first:keys, mine]
            key = qkv_ref[0:keys, part + at : part + at + HEAD_DIM]
            value = qkv_ref[0:keys, 2 * part + at : 2 * part + at + HEAD_DIM]
            grad = grad_ref[first:keys, mine]
            scores = contract_cols(key, query) + hidden
            prob = jnp.exp(scores - total_ref[head : head + 1, first:keys])
            grad_prob = contract_cols(value, grad)
            grad_score = (prob * (grad_prob - deltas[head : head + 1])).astype(BF16)
            queries.append(contract_rows(key, grad_score) * HEAD_DIM ** (-0.5))
            key_ref[0:keys, mine] += mul(grad_score, query)
            value_ref[0:keys, mine] += mul(prob.astype(BF16), grad)
        grads_ref[first:keys, :part] = jnp.concatenate(queries, 0).T.astype(BF16)
    grads_ref[:, part : 2 * part] = key_ref[...].astype(BF16)
    grads_ref[:, 2 * part :] = value_ref[...].astype(BF16)
    sums = [jnp.zeros((1, width), F32)] * 2
    for k, (x_ref, part_ref) in enumerate(zip(x_refs, part_refs)):
        at = pl.ds(pl.multiple_of((shard ^ k) * tile, tile), tile)
        grad_n = contract_cols(grads_ref[at, :], weight_ref[:, : 3 * part])
        part_ref[...] = grad_n.astype(BF16)
        normed, unused = norm_stats(x_ref[...].astype(F32))
        sums[0] += jnp.sum(grad_n * normed, 0, keepdims=True)
        sums[1] += jnp.sum(grad_n, 0, keepdims=True)
    spread_all = spread(held, width, False)
    wide = 3 * part
    owned = jnp.zeros((spread_all.shape[0], wide), F32)
    for block in range(4):
        at = slice(block * tile, (block + 1) * tile)
        turned = contract_cols(spread_all, n_ref[at, :]).astype(BF16)
        owned += mul(turned, grads_ref[at, :])
    start = -(-wide // 128) * 128 - 128
    owned_ref[:, :start] = owned[:, :start].astype(BF16)
    low = jnp.pad(owned[:, start:], ((0, 0), (0, start + 128 - wide)))
    more = gate_ref[...] + sums_in_lanes(spread_all, sums, 124)
    owned_ref[:, start : start + 128] = (low + more).astype(BF16)


def first_norm_back_body(near_ref, sib_ref, far_ref, x_ref, vector_ref, resid_grad_ref, out_ref):
    grad_n = near_ref[...].astype(F32) + sib_ref[...].astype(F32) + far_ref[...].astype(F32)
    normed, scaling = norm_stats(x_ref[...].astype(F32))
    out = resid_grad_ref[...] + norm_back(grad_n * vector_ref[0:1, :], normed, scaling)
    out_ref[...] = out.astype(BF16)


def second_sums_body(held, part, n_dp, got_ref, *refs):
    grad_refs, out_ref, gate_ref, sums_ref = refs[:3], *refs[3:]
    wide = got_ref.shape[1]
    got = got_ref[...].astype(F32).reshape(-1, 4, PAD, wide)
    total = jnp.sum(got, 0)
    last = -(-3 * part // 128) * 128
    for k in range(4):
        at = slice(k * part, (k + 1) * part)
        for m, ref in enumerate(grad_refs):
            ref[:, at] = total[k, :held, m * part : (m + 1) * part]
        out_ref[:, at] = total[k, :held, last : last + part]
    lanes = total[0] + total[1] + total[2] + total[3]
    lanes = lanes[:, last - 128 : last]
    first = 128 - 2 * n_dp
    gate_ref[...] = lanes[:held, first : first + n_dp]
    lane = iota(lanes.shape, 1)
    diagonal = iota(lanes.shape, 0) == lane
    for k, at in enumerate((124, 126, first + n_dp, first + n_dp + 2)):
        both = jnp.where((lane == at) | (lane == at + 1), lanes, 0.0)
        col_sum = jnp.sum(both, 1, keepdims=True)
        line = jnp.sum(jnp.where(diagonal, col_sum, 0.0), 0, keepdims=True)
        sums_ref[k : k + 1, :] = line[:, :held]


def layer_out_body(rows_ref, cols_ref, comb_ref, resid_ref, out_ref):
    slot = iota((cols_ref.shape[0], rows_ref.shape[0]), 1)
    out = resid_ref[...]
    for k in range(2):
        place = (slot == cols_ref[:, k : k + 1]).astype(F32).astype(BF16)
        out = out + comb_ref[:, k : k + 1] * mul(place, rows_ref[:, -out.shape[1] :])
    out_ref[...] = out.astype(BF16)


def per_device(
    tokens,
    bounds,
    routes,
    ln1_gain,
    ln1_bias,
    query_weight,
    key_weight,
    value_weight,
    output_weight,
    ln2_gain,
    ln2_bias,
    gate_new,
    gate_frozen,
    new_in,
    new_out,
    frozen_in,
    frozen_out,
    cotangent,
):
    rows, width = tokens.shape
    n_dp = lax.axis_size("dp")
    n_shard = lax.axis_size("shard")
    n_all = n_dp * n_shard
    held = query_weight.shape[0]
    padded = n_all * PAD
    group_len = rows * n_shard
    capacity = 2 * rows // n_dp
    slots = 2 * n_dp * capacity
    part = width // n_shard
    shard = lax.axis_index("shard")
    place = shard.reshape(1, 1)
    new_here = shard < n_shard // 2
    core_groups = [[2 * d + c for d in range(2 * n_dp)] for c in range(2)]
    pairs = [[0, 2], [1, 3]]
    spec_smem = pl.BlockSpec(memory_space=SMEM)
    spec_vmem = pl.BlockSpec(memory_space=VMEM)

    def swap(array, axis_groups=None):
        return lax.all_to_all(
            array, BOTH, split_axis=0, concat_axis=0, tiled=True, axis_index_groups=axis_groups
        )

    def dispatch(buffer):
        return swap(buffer.reshape(2 * n_dp, capacity, -1), core_groups).reshape(slots, -1)

    def send(array, step):
        return lax.ppermute(array, "shard", [(k, k ^ step) for k in range(n_shard)])

    def exchange(pieces):
        return [pieces[0]] + [send(piece, k) for k, piece in enumerate(pieces) if k > 0]

    x_far, x_sib = send(tokens, 2), send(tokens, 1)
    x_sib, query_weight = tie((x_sib, query_weight))

    half = width // 2
    wide = width + 128
    in_wide = -(-3 * part // 128) * 128
    last_wide = in_wide + 256
    (blocks,) = call(
        functools.partial(pack_body, part, in_wide),
        (shaped((n_dp, n_shard, PAD, in_wide + half), BF16),),
        (
            *(query_weight, key_weight, value_weight, output_weight, gate_new, gate_frozen),
            *(v[None] for v in (ln1_gain, ln1_bias, ln2_gain, ln2_bias)),
        ),
        scratch_shapes=[pltpu.VMEM((n_shard, PAD, in_wide + half), F32)],
    )
    blocks, x_far = tie((blocks, x_far))
    weights = swap(blocks.reshape(n_all, PAD, in_wide + half))
    x_last = send(x_far, 1)
    x_last, new_in, new_out, frozen_in, frozen_out = tie(
        (x_last, new_in, new_out, frozen_in, frozen_out)
    )
    x_parts = (tokens, x_sib, x_far, x_last)

    fresh, old = (new_in[0], new_out[0]), (frozen_in[0], frozen_out[0])
    own = [jnp.where(new_here, f, o) for f, o in zip(fresh, old)]
    away = jnp.stack([jnp.where(new_here, o, f) for f, o in zip(fresh, old)])
    sib_own = [send(array, 1) for array in own]

    cols, lines = call(
        functools.partial(slots_body, n_dp, capacity),
        (shaped((rows, 128), I32), shaped((8, rows), I32)),
        (routes, routes.T),
    )
    weights, x_parts, sib_own, lines, away = tie((weights, x_parts, sib_own, lines, away))
    far = lax.all_gather(away, "shard")
    in_got = weights[:, :, :in_wide].reshape(padded, in_wide)
    out_mine = weights[:, :, in_wide:].reshape(padded, half)

    w_in, vectors, n_one, qkv, *att, att_wide, log_total = call(
        functools.partial(attention_body, held),
        (
            shaped((width, in_wide), BF16),
            shaped((8, width), F32),
            shaped((group_len, width), BF16),
            shaped((group_len, in_wide), BF16),
            *[shaped((rows, part), BF16)] * 2,
            shaped((2 * rows, part), BF16),
            shaped((group_len, part), F32),
            shaped((8, group_len), F32),
        ),
        (bounds, place, in_got, *x_parts),
        in_specs=[spec_smem] * 2 + [spec_vmem] * 5,
    )
    out_sib = send(out_mine, 1)
    att_near, att_sib, att_far = att
    att_sib = send(att_sib, 1)
    att_sib, att_far = tie((att_sib, att_far))
    att_far = send(att_far, 2)
    att = att_near, att_sib, att_far, send(att_far, 1)

    w_out, resid, x_two, comb, buffer = call(
        functools.partial(router_body, held, n_dp),
        (
            shaped((width, width), BF16),
            shaped((rows, width), F32),
            shaped((rows, width), BF16),
            shaped((rows, 128), F32),
            shaped((slots, wide + width), BF16),
        ),
        (
            *(place, tokens, cotangent, *att, out_mine, out_sib),
            *(w_in, vectors, routes, lines),
        ),
        in_specs=[spec_smem] + [spec_vmem] * 12,
    )
    got = dispatch(buffer)

    back, grad_y, hidden, grad_pre = expert_call(place, got, (*own, *sib_own, far))
    back_got = dispatch(back)

    rows_t, grad_y_t = call(turn_body, (shaped((width, slots), BF16),) * 2, (got, grad_y))
    sent = weight_grads(rows_t, grad_y_t, hidden, grad_pre, 3, BF16)
    rows_t, sent = tie((rows_t, sent))
    sibs = [send(array, 1) for array in sent]
    sent_own = weight_grads(rows_t, grad_y_t, hidden, grad_pre, 2, BF16)
    rows_t, sent_own = tie((rows_t, sent_own))
    sibs_own = [send(array, 1) for array in sent_own]
    away_in, away_out = weight_grads(rows_t, grad_y_t, hidden, grad_pre, 1, BF16, sibs)
    far_in, far_out = (
        lax.all_gather(array, "shard", axis_index_groups=pairs) for array in (away_in, away_out)
    )
    own_new = weight_grads(rows_t, grad_y_t, hidden, grad_pre, 0, F32, sibs_own)
    back_got, own_new = tie((back_got, own_new))

    resid_grad, att_grad, gate_part = call(
        functools.partial(token_back_body, held, n_dp),
        (shaped((rows, width), F32), shaped((rows, width), BF16), shaped((padded, 128), F32)),
        (back_got, cols, routes, comb, cotangent, resid, x_two, w_in, vectors),
    )
    grad_far = send(att_grad, 2)
    grad_sib = send(att_grad, 1)
    layer_out = call(
        layer_out_body,
        shaped((rows, width), BF16),
        (back_got, cols, comb, resid),
    )
    grad_far, layer_out = tie((grad_far, layer_out))
    grad_last = send(grad_far, 1)
    extent = padded // n_shard
    head_grad, *out_pieces = call(
        functools.partial(projection_back_body, held),
        (shaped((group_len, part), BF16), *[shaped((extent, part), BF16)] * n_shard),
        (place, att_wide, w_out, att_grad, grad_sib, grad_far, grad_last),
        in_specs=[spec_smem] + [spec_vmem] * 6,
        scratch_shapes=[
            pltpu.VMEM((group_len, width), BF16),
            pltpu.VMEM((padded, part), BF16),
        ],
    )
    out_pieces = exchange(out_pieces)
    second_owned, *norm_part = call(
        functools.partial(attention_back_body, held),
        (shaped((padded, last_wide), BF16), *[shaped((rows, width), BF16)] * n_shard),
        (bounds, place, n_one, qkv, att_wide, log_total, w_in, gate_part, head_grad, *x_parts),
        in_specs=[spec_smem] * 2 + [spec_vmem] * 11,
        scratch_shapes=[
            pltpu.VMEM((group_len, 3 * part), BF16),
            pltpu.VMEM((group_len, part), F32),
            pltpu.VMEM((group_len, part), F32),
        ],
    )
    near_sib = send(norm_part[1], 1)
    far_sib = send(norm_part[3], 1)
    norm_far = send((norm_part[2].astype(F32) + far_sib.astype(F32)).astype(BF16), 2)
    second_owned = call(
        assemble_body,
        shaped((padded, last_wide), BF16),
        (place, second_owned, *out_pieces),
        grid=(2,),
        in_specs=[spec_smem, pl.BlockSpec(memory_space=pl.ANY)]
        + [pl.BlockSpec((extent, part), lambda c: (0, 0))] * n_shard,
        out_specs=pl.BlockSpec((padded, 128), lambda c: (0, in_wide // 128 + c)),
        input_output_aliases={1: 0},
    )
    second_got = swap(second_owned.reshape(n_all, PAD, last_wide)).reshape(padded, last_wide)
    grads_new = new_grads_call(place, own_new, far_in, far_out)
    norm_far, grads_new = tie((norm_far, grads_new))
    grad_tokens = call(
        first_norm_back_body,
        shaped((rows, width), BF16),
        (norm_part[0], near_sib, norm_far, tokens, vectors, resid_grad),
    )
    *grads_in, grad_out, grad_gate, ln_sums = call(
        functools.partial(second_sums_body, held, part, n_dp),
        (*[shaped((held, width), F32)] * 4, shaped((held, n_dp), F32), shaped((4, held), F32)),
        (second_got,),
    )
    return (
        *(layer_out, grad_tokens, *grads_in, grad_out),
        *(ln_sums[0], ln_sums[1], ln_sums[2], ln_sums[3]),
        *(grad_gate, *grads_new),
    )


def solution(mesh):
    flat = P(BOTH)
    lines = P(BOTH, None)
    in_specs = (
        (lines, P("dp", None), lines)
        + (flat, flat)
        + (lines,) * 4
        + (flat, flat, lines, lines)
        + (P("dp", None, "shard"), P("dp", "shard", None)) * 2
        + (lines,)
    )
    out_specs = (
        (lines,) * 6
        + (flat,) * 4
        + (lines, P("dp", None, "shard"), P("dp", "shard", None))
    )
    return jax.shard_map(
        per_device, mesh=mesh, in_specs=in_specs, out_specs=out_specs, check_vma=False
    )
```

time: 1060 us -> 376 us (0.35)
  waiting for transfers between devices: 689 us -> 90.7 us
  Pallas kernels: 0 us -> 136 us
  matrix products: 135 us -> 0 us
  local copies, waits for them, and re-layouts: 97.3 us -> 12.8 us
  starting transfers between devices: 13.2 us -> 53.5 us
  other arithmetic: 43.6 us -> 7.85 us
    all_gather x4 -> x3, waiting for transfers between devices: 433 us -> 23.2 us  [the longest x2 17 us: per_device(): lax.all_gather(array, 'shard', axis_index_groups=pairs)]
    unnamed x9 -> x3, waiting for transfers between devices: 167 us -> 0.05 us
    pallas_call x0 -> x18, Pallas kernels: none -> 136 us  [call(): pl.pallas_call(body, out_shape=out_shapes, compiler_params=pltpu.Compiler...]
    dot_general x36 -> x0, matrix products: 135 us -> none  [the longest x9 39.1 us: contract_cols(): lax.dot_general(left, right, (((1,), (1,)), ((), ())), preferred_element_...]
    reduce_scatter x3 -> x0, waiting for transfers between devices: 72.3 us -> none  [the longest x1 54 us: per_device(): lax.psum_scatter(grad_out_new.astype(jnp.bfloat16), 'shard', scatter_dime...]
    ppermute x0 -> x22, waiting for transfers between devices: none -> 49.9 us  [send(): return lax.ppermute(array, 'shard', [(k, k ^ step) for k in range(n_shard)])]
    ppermute x0 -> x22, starting transfers between devices: none -> 26.3 us  [send(): return lax.ppermute(array, 'shard', [(k, k ^ step) for k in range(n_shard)])]
    unnamed x177 -> x57, local copies, waits for them, and re-layouts: 27.6 us -> 10.2 us
  transfers between devices with their start and end apart: 10 -> 28, of which waited for: 9 -> 13; matrix products, arithmetic and copies ran while one was open for 18% -> 3% of each run, Pallas kernels for 0% -> 28%
where the time goes in v1:
time: 376 us; the launch traced here: 372 us
  Pallas kernels  136 us (36%)
  waiting for transfers between devices  90.7 us (24%)
  blocking collectives  56.3 us (15%)
  starting transfers between devices  53.5 us (14%)
  between operations  14.5 us (4%)
  local copies, waits for them, and re-layouts  12.8 us (3%)
  other arithmetic  7.85 us (2%)
    pallas_call x18, Pallas kernels, call(): pl.pallas_call(body, out_shape=out_shapes, compiler_params=pltpu.Compiler...  136 us
    all_to_all x1, blocking collectives, swap(): lax.all_to_all(array, BOTH, split_axis=0, concat_axis=0, tiled=True, axis...  56.3 us
    ppermute x22, waiting for transfers between devices, send(): return lax.ppermute(array, 'shard', [(k, k ^ step) for k in range(n_shard)])  49.9 us
    all_to_all x3, starting transfers between devices, swap(): lax.all_to_all(array, BOTH, split_axis=0, concat_axis=0, tiled=True, axis...  27.1 us
    ppermute x22, starting transfers between devices, send(): return lax.ppermute(array, 'shard', [(k, k ^ step) for k in range(n_shard)])  26.3 us
    all_to_all x3, waiting for transfers between devices, swap(): lax.all_to_all(array, BOTH, split_axis=0, concat_axis=0, tiled=True, axis...  17.5 us
    all_gather x2, waiting for transfers between devices, per_device(): lax.all_gather(array, 'shard', axis_index_groups=pairs)  17 us
    unnamed x57, local copies, waits for them, and re-layouts  10.2 us
  transfers between devices with their start and end apart: 28, of which 13 were waited for; matrix products, arithmetic and copies ran while one was open for 3% of the time, Pallas kernels for 28%

profile of v1, /device:TPU:1, one launch (start us, length us, event | category | flops | bytes accessed | tf_op | source)
XLA Modules:
  0.0 372.0 jit_solution(874792822058787674)
XLA Ops:
  8.7 3.0 collective-permute-start.1
  14.1 7.0 %collective-permute-done.1.refs_2_ = bf16[256,768]{1,0:T(8,128)(2,1)S(1)} collective-permute-done((bf16[256,768]{1,0:T(8,128)(2,1)}, bf16[256,768]{1,0:T(8,128)(2,1)S(1)}, u32[]{:S(2)}, u32[]{:S(2)}) %collective-permute-start.1) | collective-permute-done | bytes 393248 | tf_op jit(solution)/shard_map/ppermute | solution.py:718
  22.0 10.8 %all-to-all-start = ((bf16[128,8,1024]{2,1,0:T(8,128)(2,1)}), bf16[128,8,1024]{2,1,0:T(8,128)(2,1)S(1)}, u32[]{:S(2)}, u32[]{:S(2)}) async-start(bf16[128,8,1024]{2,1,0:T(8,128)(2,1)} %bitcast.37), calls=%async_computation | async-start | bytes 4194304 | tf_op jit(solution)/shard_map/all_to_all | solution.py:710
  32.9 3.0 broadcast_select_fusion.1
  41.5 3.2 pad_maximum_fusion
  44.8 17.5 %all-to-all-done = bf16[128,8,1024]{2,1,0:T(8,128)(2,1)S(1)} async-done(((bf16[128,8,1024]{2,1,0:T(8,128)(2,1)}), bf16[128,8,1024]{2,1,0:T(8,128)(2,1)S(1)}, u32[]{:S(2)}, u32[]{:S(2)}) %all-to-all-start) | async-done | bytes 2097184 | tf_op jit(solution)/shard_map/all_to_all | solution.py:710
  65.2 13.5 %shard_map.275 = (bf16[768,640]{1,0:T(8,128)(2,1)}, f32[8,768]{1,0:T(8,128)}, bf16[1024,768]{1,0:T(8,128)(2,1)}, bf16[1024,640]{1,0:T(8,128)(2,1)}, bf16[256,192...) custom-call(s32[1,2]{1,0:T(1,128)} %bounds_ref.3, ...), custom_call_target="tpu_custom_call" | custom-call | flops 1 | bytes 1 | tf_op jit(solution)/shard_map/pallas_call | solution.py:88
  81.7 14.1 %collective-permute-done.6.far_ref = bf16[512,192]{1,0:T(8,128)(2,1)S(1)} collective-permute-done((bf16[512,192]{1,0:T(8,128)(2,1)}, bf16[512,192]{1,0:T(8,128)(2,1)S(1)}, u32[]{:S(2)}, u32[]{:S(2)}) %collective-permute-start.6) | collective-permute-done | bytes 196640 | tf_op jit(solution)/shard_map/ppermute | solution.py:718
  99.3 8.8 %shard_map.276 = (bf16[768,768]{1,0:T(8,128)(2,1)}, f32[256,768]{1,0:T(8,128)}, bf16[256,768]{1,0:T(8,128)(2,1)}, f32[256,128]{1,0:T(8,128)}, bf16[1024,1664]{1,0:T(8,128)(2,1)}) custom-call(s32[1,1]{1,0:T(1,128)} %bitcast.shard_ref, bf16[256,768]{1,0:T(8,128)(2,1)} %x_ref.3, bf16[256,768]{1,0:T(8,128)(2,1)} %grad_ref.3, ...), custom_call_target="tpu_custom_call" | custom-call | flops 1 | bytes 1 | tf_op jit(solution)/shard_map/pallas_call | solution.py:88
  108.0 56.3 %all_to_all.20 = bf16[64,16,1664]{2,1,0:T(8,128)(2,1)} all-to-all(bf16[64,16,1664]{2,1,0:T(8,128)(2,1)} %bitcast.41), channel_id=1, replica_groups={{0,2,4,6,8,10,12,14,16,18,20,22,24,26,28,30,32,34,36,38,40,42,44,46,48,..., dimensions={0} | all-to-all | bytes 6815744 | tf_op jit(solution)/shard_map/all_to_all | solution.py:710
  164.3 6.2 %all-gather.7.cloned.1.call-done = bf16[8,768,768]{2,1,0:T(8,128)(2,1)} async-done(((bf16[2,768,768]{2,1,0:T(8,128)(2,1)}), bf16[8,768,768]{2,1,0:T(8,128)(2,1)}) %all-gather.7.cloned.1.call-update) | async-done | bytes 9437200 | tf_op jit(solution)/shard_map/all_gather | solution.py:758
  170.5 29.8 %shard_map.277 = (bf16[1024,1664]{1,0:T(8,128)(2,1)}, bf16[1024,768]{1,0:T(8,128)(2,1)}, bf16[1024,3072]{1,0:T(8,128)(2,1)}, bf16[1024,3072]{1,0:T(8,128)(2,1)}) custom-call(s32[1,1]{1,0:T(1,128)} %bitcast.shard_ref, bf16[1024,1664]{1,0:T(8,128)(2,1)} %bitcast.32, bf16[768,768]{1,0:T(8,128)(2,1)} %copy-done.2, bf16[768,768]{1,0:T(8,128)(2,1)} %get-tuple-element.186.refs_1_, ...), custom_call_target="tpu_custom_call" | custom-call | flops 1 | bytes 1 | tf_op jit(solution)/shard_map/pallas_call | solution.py:88
  200.3 8.4 %all-to-all-start.2 = ((bf16[64,16,1664]{2,1,0:T(8,128)(2,1)}), bf16[64,16,1664]{2,1,0:T(8,128)(2,1)S(1)}, u32[]{:S(2)}, u32[]{:S(2)}) async-start(bf16[64,16,1664]{2,1,0:T(8,128)(2,1)} %bitcast.40), calls=%async_computation.2 | async-start | bytes 6815744 | tf_op jit(solution)/shard_map/all_to_all | solution.py:710
  208.7 4.6 %shard_map.278 = (bf16[768,1024]{1,0:T(8,128)(2,1)}, bf16[768,1024]{1,0:T(8,128)(2,1)}) custom-call(bf16[1024,1664]{1,0:T(8,128)(2,1)} %bitcast.33, bf16[1024,768]{1,0:T(8,128)(2,1)} %get-tuple-element.126.grad_y_ref), custom_call_target="tpu_custom_call" | custom-call | flops 1 | bytes 1 | tf_op jit(solution)/shard_map/pallas_call | solution.py:88
  213.3 6.7 %shard_map.279 = (bf16[768,768]{1,0:T(8,128)(2,1)}, bf16[768,768]{1,0:T(8,128)(2,1)}) custom-call(bf16[768,1024]{1,0:T(8,128)(2,1)} %get-tuple-element.136.rows_t_ref, bf16[768,1024]{1,0:T(8,128)(2,1)} %get-tuple-element.128.grad_y_t_ref, bf16[1024,3072]{1,0:T(8,128)(2,1)} %get-tuple-element.129.hidden_ref, bf16[1024,3072]{1,0:T(8,128)(2,1)} %get-tuple-element.130.grad_pre_ref), custom_call_target="tpu_custom_call" | custom-call | flops 1 | bytes 1 | tf_op jit(solution)/shard_map/pallas_call | solution.py:88
  220.5 6.8 %shard_map.280 = (bf16[768,768]{1,0:T(8,128)(2,1)}, bf16[768,768]{1,0:T(8,128)(2,1)}) custom-call(bf16[768,1024]{1,0:T(8,128)(2,1)} %get-tuple-element.136.rows_t_ref, bf16[768,1024]{1,0:T(8,128)(2,1)} %get-tuple-element.128.grad_y_t_ref, bf16[1024,3072]{1,0:T(8,128)(2,1)} %get-tuple-element.129.hidden_ref, bf16[1024,3072]{1,0:T(8,128)(2,1)} %get-tuple-element.130.grad_pre_ref), custom_call_target="tpu_custom_call" | custom-call | flops 1 | bytes 1 | tf_op jit(solution)/shard_map/pallas_call | solution.py:88
  229.5 7.4 %shard_map.286 = (bf16[768,768]{1,0:T(8,128)(2,1)}, bf16[768,768]{1,0:T(8,128)(2,1)}) custom-call(bf16[768,1024]{1,0:T(8,128)(2,1)} %get-tuple-element.136.rows_t_ref, bf16[768,1024]{1,0:T(8,128)(2,1)} %get-tuple-element.128.grad_y_t_ref, bf16[1024,3072]{1,0:T(8,128)(2,1)} %get-tuple-element.129.hidden_ref, ...), custom_call_target="tpu_custom_call" | custom-call | flops 1 | bytes 1 | tf_op jit(solution)/shard_map/pallas_call | solution.py:88
  237.5 2.6 collective-permute-done.9.refs_0_
  242.8 8.6 %shard_map.281 = (f32[768,768]{1,0:T(8,128)}, f32[768,768]{1,0:T(8,128)}) custom-call(bf16[768,1024]{1,0:T(8,128)(2,1)} %get-tuple-element.136.rows_t_ref, bf16[768,1024]{1,0:T(8,128)(2,1)} %get-tuple-element.128.grad_y_t_ref, bf16[1024,3072]{1,0:T(8,128)(2,1)} %get-tuple-element.129.hidden_ref, bf16[1024,3072]{1,0:T(8,128)(2,1)} %get-tuple-element.130.grad_pre_ref, ...), custom_call_target="tpu_custom_call" | custom-call | flops 1 | bytes 1 | tf_op jit(solution)/shard_map/pallas_call | solution.py:88
  253.1 6.8 %shard_map.282 = (f32[256,768]{1,0:T(8,128)}, bf16[256,768]{1,0:T(8,128)(2,1)}, f32[1024,128]{1,0:T(8,128)}) custom-call(bf16[1024,1664]{1,0:T(8,128)(2,1)} %bitcast.34, s32[256,128]{1,0:T(8,128)} %get-tuple-element.142.cols_ref, s32[256,2]{1,0:T(8,128)} %copy.35.routes_ref, f32[256,128]{1,0:T(8,128)} %get-tuple-element.143.comb_ref, ...), custom_call_target="tpu_custom_call" | custom-call | flops 1 | bytes 1 | tf_op jit(solution)/shard_map/pallas_call | solution.py:88
  259.9 2.8 collective-permute-start.11
  262.7 4.1 %shard_map.283 = bf16[256,768]{1,0:T(8,128)(2,1)} custom-call(bf16[1024,1664]{1,0:T(8,128)(2,1)} %bitcast.35, s32[256,128]{1,0:T(8,128)} %get-tuple-element.142.cols_ref, f32[256,128]{1,0:T(8,128)} %get-tuple-element.143.comb_ref, f32[256,768]{1,0:T(8,128)} %get-tuple-element.144.resid_ref), custom_call_target="tpu_custom_call" | custom-call | flops 1 | bytes 1 | tf_op jit(solution)/shard_map/pallas_call | solution.py:88
  267.5 13.0 %collective-permute-done.11.far_ref = bf16[256,768]{1,0:T(8,128)(2,1)S(1)} collective-permute-done((bf16[256,768]{1,0:T(8,128)(2,1)}, bf16[256,768]{1,0:T(8,128)(2,1)S(1)}, u32[]{:S(2)}, u32[]{:S(2)}) %collective-permute-start.11) | collective-permute-done | bytes 393248 | tf_op jit(solution)/shard_map/ppermute | solution.py:718
  280.5 2.7 collective-permute-start.13
  285.2 4.1 %shard_map.284 = (bf16[1024,192]{1,0:T(8,128)(2,1)}, bf16[256,192]{1,0:T(8,128)(2,1)}, bf16[256,192]{1,0:T(8,128)(2,1)}, bf16[256,192]{1,0:T(8,128)(2,1)}, bf16[256,192]{1,0:T(8,128)(2,1)}) custom-call(s32[1,1]{1,0:T(1,128)} %bitcast.shard_ref, f32[1024,192]{1,0:T(8,128)} %get-tuple-element.150.att_ref, bf16[768,768]{1,0:T(8,128)(2,1)} %get-tuple-element.153.weight_ref, ...), custom_call_target="tpu_custom_call" | custom-call | flops 1 | bytes 1 | tf_op jit(solution)/shard_map/pallas_call | solution.py:88
  293.3 17.1 %shard_map.285 = (bf16[1024,896]{1,0:T(8,128)(2,1)}, bf16[256,768]{1,0:T(8,128)(2,1)}, bf16[256,768]{1,0:T(8,128)(2,1)}, bf16[256,768]{1,0:T(8,128)(2,1)}, bf16[256,768]{1,0:T(8,128)(2,1)}) custom-call(s32[1,2]{1,0:T(1,128)} %bounds_ref.3, s32[1,1]{1,0:T(1,128)} %bitcast.shard_ref, bf16[1024,768]{1,0:T(8,128)(2,1)} %get-tuple-element.148.n_ref, ...), custom_call_target="tpu_custom_call" | custom-call | flops 1 | bytes 1 | tf_op jit(solution)/shard_map/pallas_call | solution.py:88
  313.2 7.9 %all-to-all-start.3 = ((bf16[128,8,896]{2,1,0:T(8,128)(2,1)}), bf16[128,8,896]{2,1,0:T(8,128)(2,1)S(1)}, u32[]{:S(2)}, u32[]{:S(2)}) async-start(bf16[128,8,896]{2,1,0:T(8,128)(2,1)} %bitcast.39), calls=%async_computation.3 | async-start | bytes 3670016 | tf_op jit(solution)/shard_map/all_to_all | solution.py:710
  326.6 17.0 %all-gather.11.cloned.1.call-done = bf16[1536,768]{1,0:T(8,128)(2,1)} async-done(((bf16[768,768]{1,0:T(8,128)(2,1)}), bf16[1536,768]{1,0:T(8,128)(2,1)}) %all-gather.11.cloned.1.call-update) | async-done | bytes 2359312 | tf_op jit(solution)/shard_map/all_gather | solution.py:813
  343.7 6.2 %shard_map.287 = (f32[1,768,768]{2,1,0:T(8,128)}, f32[1,768,768]{2,1,0:T(8,128)}) custom-call(s32[1,1]{1,0:T(1,128)} %bitcast.shard_ref, f32[768,768]{1,0:T(8,128)} %get-tuple-element.160.in_ref, f32[768,768]{1,0:T(8,128)} %get-tuple-element.161.out_ref, bf16[2,768,768]{2,1,0:T(8,128)(2,1)} %bitcast.42, bf16[2,768,768]{2,1,0:T(8,128)(2,1)} %bitcast.43), custom_call_target="tpu_custom_call" | custom-call | flops 1 | bytes 1 | tf_op jit(solution)/shard_map/pallas_call | solution.py:88
  349.8 6.1 %collective-permute-done.16.far_ref = bf16[256,768]{1,0:T(8,128)(2,1)S(1)} collective-permute-done((bf16[256,768]{1,0:T(8,128)(2,1)S(1)}, bf16[256,768]{1,0:T(8,128)(2,1)S(1)}, u32[]{:S(2)}, u32[]{:S(2)}) %collective-permute-start.16) | collective-permute-done | bytes 393248 | tf_op jit(solution)/shard_map/ppermute | solution.py:718
  356.9 3.0 shard_map.288
  361.1 2.5 shard_map.290
  (110 shorter events, 46.0 us)
Async XLA Ops:
  7.2 4.5 %collective-permute-start = (bf16[256,768]{1,0:T(8,128)(2,1)}, bf16[256,768]{1,0:T(8,128)(2,1)}, u32[]{:S(2)}, u32[]{:S(2)}) collective-permute-start(bf16[256,768]{1,0:T(8,128)(2,1)} %x_ref.3), channel_id=1, source_target_pairs={{0,1},{1,0},{2,3},{3,2},{4,5},{5,4},{6,7},{7,6},{8,9},{9,8},{10,11... | collective-permute-start | bytes 1179656 | tf_op jit(solution)/shard_map/ppermute | solution.py:718
  8.7 12.4 %collective-permute-start.1 = (bf16[256,768]{1,0:T(8,128)(2,1)}, bf16[256,768]{1,0:T(8,128)(2,1)S(1)}, u32[]{:S(2)}, u32[]{:S(2)}) collective-permute-start(bf16[256,768]{1,0:T(8,128)(2,1)} %x_ref.3), channel_id=1, source_target_pairs={{0,2},{1,3},{2,0},{3,1},{4,6},{5,7},{6,4},{7,5},{8,10},{9,11},{10,... | collective-permute-start | bytes 1179656 | tf_op jit(solution)/shard_map/ppermute | solution.py:718
  21.1 11.7 %collective-permute-start.2 = (bf16[256,768]{1,0:T(8,128)(2,1)S(1)}, bf16[256,768]{1,0:T(8,128)(2,1)}, u32[]{:S(2)}, u32[]{:S(2)}) collective-permute-start(bf16[256,768]{1,0:T(8,128)(2,1)S(1)} %collective-permute-done.1.refs_2_), channel_id=1, source_target_pairs={{0,1},{1,0},{2,3},{3,2},{4,5},{5,4},{6,7},{7,6},{8,9},{9,8},{10,11... | collective-permute-start | bytes 1179656 | tf_op jit(solution)/shard_map/ppermute | solution.py:718
  22.0 40.3 %all-to-all-start = ((bf16[128,8,1024]{2,1,0:T(8,128)(2,1)}), bf16[128,8,1024]{2,1,0:T(8,128)(2,1)S(1)}, u32[]{:S(2)}, u32[]{:S(2)}) async-start(bf16[128,8,1024]{2,1,0:T(8,128)(2,1)} %bitcast.37), calls=%async_computation | async-start | bytes 4194304 | tf_op jit(solution)/shard_map/all_to_all | solution.py:710
  32.8 137.7 %all-gather.7.cloned.1.call-start = ((), (), s32[]{:S(2)}) async-start(), calls=%async_computation.4 | async-start | bytes 11796480 | tf_op jit(solution)/shard_map/all_gather | solution.py:758
  35.8 9.0 %collective-permute-start.3 = (bf16[768,768]{1,0:T(8,128)(2,1)S(1)}, bf16[768,768]{1,0:T(8,128)(2,1)}, u32[]{:S(2)}, u32[]{:S(2)}) collective-permute-start(bf16[768,768]{1,0:T(8,128)(2,1)S(1)} %get-tuple-element.184.refs_0_), channel_id=1, source_target_pairs={{0,1},{1,0},{2,3},{3,2},{4,5},{5,4},{6,7},{7,6},{8,9},{9,8},{10,11... | collective-permute-start | bytes 3538952 | tf_op jit(solution)/shard_map/ppermute | solution.py:718
  38.4 6.4 %collective-permute-start.4 = (bf16[768,768]{1,0:T(8,128)(2,1)}, bf16[768,768]{1,0:T(8,128)(2,1)}, u32[]{:S(2)}, u32[]{:S(2)}) collective-permute-start(bf16[768,768]{1,0:T(8,128)(2,1)} %get-tuple-element.186.refs_1_), channel_id=1, source_target_pairs={{0,1},{1,0},{2,3},{3,2},{4,5},{5,4},{6,7},{7,6},{8,9},{9,8},{10,11... | collective-permute-start | bytes 3538952 | tf_op jit(solution)/shard_map/ppermute | solution.py:718
  62.4 35.9 %collective-permute-start.8 = (bf16[1024,384]{1,0:T(8,128)(2,1)S(1)}, bf16[1024,384]{1,0:T(8,128)(2,1)S(1)}, u32[]{:S(2)}, u32[]{:S(2)}) collective-permute-start(bf16[1024,384]{1,0:T(8,128)(2,1)S(1)} %slice_bitcast_fusion.1.mine_ref), channel_id=1, source_target_pairs={{0,1},{1,0},{2,3},{3,2},{4,5},{5,4},{6,7},{7,6},{8,9},{9,8},{10,11... | collective-permute-start | bytes 2359304 | tf_op jit(solution)/shard_map/ppermute | solution.py:718
  78.7 1.6 collective-permute-start.5
  80.3 18.1 %copy-start.24 = (bf16[256,192]{1,0:T(8,128)(2,1)}, bf16[256,192]{1,0:T(8,128)(2,1)S(1)}, u32[]{:S(2)}) copy-start(bf16[256,192]{1,0:T(8,128)(2,1)S(1)} %collective-permute-done.5.sib_ref) | copy-start | bytes 294916
  80.3 15.5 %collective-permute-start.6 = (bf16[512,192]{1,0:T(8,128)(2,1)}, bf16[512,192]{1,0:T(8,128)(2,1)S(1)}, u32[]{:S(2)}, u32[]{:S(2)}) collective-permute-start(bf16[512,192]{1,0:T(8,128)(2,1)} %get-tuple-element.117), channel_id=1, source_target_pairs={{0,2},{1,3},{2,0},{3,1},{4,6},{5,7},{6,4},{7,5},{8,10},{9,11},{10,... | collective-permute-start | bytes 589832 | tf_op jit(solution)/shard_map/ppermute | solution.py:718
  95.8 2.5 collective-permute-start.7
  200.3 51.1 %all-to-all-start.2 = ((bf16[64,16,1664]{2,1,0:T(8,128)(2,1)}), bf16[64,16,1664]{2,1,0:T(8,128)(2,1)S(1)}, u32[]{:S(2)}, u32[]{:S(2)}) async-start(bf16[64,16,1664]{2,1,0:T(8,128)(2,1)} %bitcast.40), calls=%async_computation.2 | async-start | bytes 6815744 | tf_op jit(solution)/shard_map/all_to_all | solution.py:710
  208.7 118.0 %all-gather.9.cloned.1.call-start = ((), (), s32[]{:S(2)}) async-start(), calls=%async_computation.5 | async-start | bytes 3538944 | tf_op jit(solution)/shard_map/all_gather | solution.py:813
  219.9 7.5 %collective-permute-start.17 = (bf16[768,768]{1,0:T(8,128)(2,1)}, bf16[768,768]{1,0:T(8,128)(2,1)S(1)}, u32[]{:S(2)}, u32[]{:S(2)}) collective-permute-start(bf16[768,768]{1,0:T(8,128)(2,1)} %get-tuple-element.162), channel_id=1, source_target_pairs={{0,1},{1,0},{2,3},{3,2},{4,5},{5,4},{6,7},{7,6},{8,9},{9,8},{10,11... | collective-permute-start | bytes 3538952 | tf_op jit(solution)/shard_map/ppermute | solution.py:718
  220.5 6.9 %collective-permute-start.18 = (bf16[768,768]{1,0:T(8,128)(2,1)}, bf16[768,768]{1,0:T(8,128)(2,1)S(1)}, u32[]{:S(2)}, u32[]{:S(2)}) collective-permute-start(bf16[768,768]{1,0:T(8,128)(2,1)} %get-tuple-element.163), channel_id=1, source_target_pairs={{0,1},{1,0},{2,3},{3,2},{4,5},{5,4},{6,7},{7,6},{8,9},{9,8},{10,11... | collective-permute-start | bytes 3538952 | tf_op jit(solution)/shard_map/ppermute | solution.py:718
  236.8 106.8 %all-gather.11.cloned.1.call-start = ((), (), s32[]{:S(2)}) async-start(), calls=%async_computation.6 | async-start | bytes 3538944 | tf_op jit(solution)/shard_map/all_gather | solution.py:813
  236.9 3.2 collective-permute-start.9
  237.4 4.4 %collective-permute-start.10 = (bf16[768,768]{1,0:T(8,128)(2,1)}, bf16[768,768]{1,0:T(8,128)(2,1)S(1)}, u32[]{:S(2)}, u32[]{:S(2)}) collective-permute-start(bf16[768,768]{1,0:T(8,128)(2,1)} %get-tuple-element.138), channel_id=1, source_target_pairs={{0,1},{1,0},{2,3},{3,2},{4,5},{5,4},{6,7},{7,6},{8,9},{9,8},{10,11... | collective-permute-start | bytes 3538952 | tf_op jit(solution)/shard_map/ppermute | solution.py:718
  259.9 20.6 %collective-permute-start.11 = (bf16[256,768]{1,0:T(8,128)(2,1)}, bf16[256,768]{1,0:T(8,128)(2,1)S(1)}, u32[]{:S(2)}, u32[]{:S(2)}) collective-permute-start(bf16[256,768]{1,0:T(8,128)(2,1)} %get-tuple-element.146.near_ref), channel_id=1, source_target_pairs={{0,2},{1,3},{2,0},{3,1},{4,6},{5,7},{6,4},{7,5},{8,10},{9,11},{10,... | collective-permute-start | bytes 1179656 | tf_op jit(solution)/shard_map/ppermute | solution.py:718
  266.8 16.3 %collective-permute-start.12 = (bf16[256,768]{1,0:T(8,128)(2,1)S(1)}, bf16[256,768]{1,0:T(8,128)(2,1)S(1)}, u32[]{:S(2)}, u32[]{:S(2)}) collective-permute-start(bf16[256,768]{1,0:T(8,128)(2,1)S(1)} %copy-done.12), channel_id=1, source_target_pairs={{0,1},{1,0},{2,3},{3,2},{4,5},{5,4},{6,7},{7,6},{8,9},{9,8},{10,11... | collective-permute-start | bytes 1179656 | tf_op jit(solution)/shard_map/ppermute | solution.py:718
  280.5 4.0 %collective-permute-start.13 = (bf16[256,768]{1,0:T(8,128)(2,1)S(1)}, bf16[256,768]{1,0:T(8,128)(2,1)S(1)}, u32[]{:S(2)}, u32[]{:S(2)}) collective-permute-start(bf16[256,768]{1,0:T(8,128)(2,1)S(1)} %collective-permute-done.11.far_ref), channel_id=1, source_target_pairs={{0,1},{1,0},{2,3},{3,2},{4,5},{5,4},{6,7},{7,6},{8,9},{9,8},{10,11... | collective-permute-start | bytes 1179656 | tf_op jit(solution)/shard_map/ppermute | solution.py:718
  289.4 21.0 %collective-permute-start.19 = (bf16[256,192]{1,0:T(8,128)(2,1)}, bf16[256,192]{1,0:T(8,128)(2,1)S(1)}, u32[]{:S(2)}, u32[]{:S(2)}) collective-permute-start(bf16[256,192]{1,0:T(8,128)(2,1)} %get-tuple-element.172), channel_id=1, source_target_pairs={{0,1},{1,0},{2,3},{3,2},{4,5},{5,4},{6,7},{7,6},{8,9},{9,8},{10,11... | collective-permute-start | bytes 294920 | tf_op jit(solution)/shard_map/ppermute | solution.py:718
  289.7 20.7 %collective-permute-start.20 = (bf16[256,192]{1,0:T(8,128)(2,1)}, bf16[256,192]{1,0:T(8,128)(2,1)S(1)}, u32[]{:S(2)}, u32[]{:S(2)}) collective-permute-start(bf16[256,192]{1,0:T(8,128)(2,1)} %get-tuple-element.173), channel_id=1, source_target_pairs={{0,2},{1,3},{2,0},{3,1},{4,6},{5,7},{6,4},{7,5},{8,10},{9,11},{10,... | collective-permute-start | bytes 294920 | tf_op jit(solution)/shard_map/ppermute | solution.py:718
  291.5 19.0 %collective-permute-start.21 = (bf16[256,192]{1,0:T(8,128)(2,1)}, bf16[256,192]{1,0:T(8,128)(2,1)S(1)}, u32[]{:S(2)}, u32[]{:S(2)}) collective-permute-start(bf16[256,192]{1,0:T(8,128)(2,1)} %get-tuple-element.174), channel_id=1, source_target_pairs={{0,3},{1,2},{2,1},{3,0},{4,7},{5,6},{6,5},{7,4},{8,11},{9,10},{10,... | collective-permute-start | bytes 294920 | tf_op jit(solution)/shard_map/ppermute | solution.py:718
  313.2 8.0 %copy-start.27 = (bf16[256,768]{1,0:T(8,128)(2,1)S(1)}, bf16[256,768]{1,0:T(8,128)(2,1)}, u32[]{:S(2)}) copy-start(bf16[256,768]{1,0:T(8,128)(2,1)} %get-tuple-element.159) | copy-start | bytes 1179652
  313.2 10.5 %copy-start.16 = (bf16[256,768]{1,0:T(8,128)(2,1)S(1)}, bf16[256,768]{1,0:T(8,128)(2,1)}, u32[]{:S(2)}) copy-start(bf16[256,768]{1,0:T(8,128)(2,1)} %get-tuple-element.158) | copy-start | bytes 1179652
  313.2 12.8 %copy-start.26 = (bf16[256,768]{1,0:T(8,128)(2,1)S(1)}, bf16[256,768]{1,0:T(8,128)(2,1)}, u32[]{:S(2)}) copy-start(bf16[256,768]{1,0:T(8,128)(2,1)} %get-tuple-element.157) | copy-start | bytes 1179652
  313.2 46.7 %all-to-all-start.3 = ((bf16[128,8,896]{2,1,0:T(8,128)(2,1)}), bf16[128,8,896]{2,1,0:T(8,128)(2,1)S(1)}, u32[]{:S(2)}, u32[]{:S(2)}) async-start(bf16[128,8,896]{2,1,0:T(8,128)(2,1)} %bitcast.39), calls=%async_computation.3 | async-start | bytes 3670016 | tf_op jit(solution)/shard_map/all_to_all | solution.py:710
  321.1 2.5 collective-permute-start.15
  323.7 32.2 %collective-permute-start.16 = (bf16[256,768]{1,0:T(8,128)(2,1)S(1)}, bf16[256,768]{1,0:T(8,128)(2,1)S(1)}, u32[]{:S(2)}, u32[]{:S(2)}) collective-permute-start(bf16[256,768]{1,0:T(8,128)(2,1)S(1)} %add_convert_fusion), channel_id=1, source_target_pairs={{0,2},{1,3},{2,0},{3,1},{4,6},{5,7},{6,4},{7,5},{8,10},{9,11},{10,... | collective-permute-start | bytes 1179656 | tf_op jit(solution)/shard_map/ppermute | solution.py:718
  326.0 30.0 %collective-permute-start.14 = (bf16[256,768]{1,0:T(8,128)(2,1)S(1)}, bf16[256,768]{1,0:T(8,128)(2,1)S(1)}, u32[]{:S(2)}, u32[]{:S(2)}) collective-permute-start(bf16[256,768]{1,0:T(8,128)(2,1)S(1)} %copy-done.26), channel_id=1, source_target_pairs={{0,1},{1,0},{2,3},{3,2},{4,5},{5,4},{6,7},{7,6},{8,9},{9,8},{10,11... | collective-permute-start | bytes 1179656 | tf_op jit(solution)/shard_map/ppermute | solution.py:718
  (24 other events, 43.1 us)
Sparse Core Ops, SparseCore 0:
  62.4 108.0 all-gather.6
  237.0 49.5 all-gather.8
  288.2 55.3 all-gather.10

commit v2 on v1

--- a/solution.py
+++ b/solution.py
@@ -170,14 +170,24 @@
     return jnp.where(seen, 0.0, -1e30)
 
 
-def attention_body(held, bounds_ref, shard_ref, got_ref, *refs):
-    x_refs, (weight_ref, vector_ref, n_ref, qkv_ref), refs = refs[:4], refs[4:8], refs[8:]
+def prepare_body(held, shard_ref, *refs):
+    x_refs, normed_ref, spread_ref = refs[:4], refs[4], refs[5]
+    tile, width = x_refs[0].shape
+    for k, x_ref in enumerate(x_refs):
+        at = pl.ds(pl.multiple_of((shard_ref[0, 0] ^ k) * tile, tile), tile)
+        normed_ref[at, :], unused = norm_stats(x_ref[...].astype(F32))
+    spread_ref[...] = spread(held, width, True)
+
+
+def attention_body(held, bounds_ref, shard_ref, got_ref, normed_ref, spread_ref, *refs):
+    (weight_ref, vector_ref, n_ref, qkv_ref), refs = refs[:4], refs[4:]
     near_ref, sib_ref, far_ref, att_wide_ref, total_ref = refs
-    tile, width = x_refs[0].shape
+    width = normed_ref.shape[1]
+    tile = normed_ref.shape[0] // 4
     part = att_wide_ref.shape[1]
     shard = shard_ref[0, 0]
     got = got_ref[...]
-    weight_ref[...] = mul(spread(held, width, True), got).astype(BF16)
+    weight_ref[...] = mul(spread_ref[...], got).astype(BF16)
     lanes, last = got[:, :128], got[:, got.shape[1] - 128 :]
     first = 3 * part - (got.shape[1] - 128)
     gain = vector_rows(lanes, held, width, held)
@@ -188,10 +198,9 @@
     vector_ref[...] = jnp.where(
         sub == 3, vector_rows(last, held, width, held + 1, first), vectors
     )
-    for k, x_ref in enumerate(x_refs):
-        at = pl.ds(pl.multiple_of((shard ^ k) * tile, tile), tile)
-        normed, unused = norm_stats(x_ref[...].astype(F32))
-        n_one = (normed * gain + bias).astype(BF16)
+    for block in range(4):
+        at = slice(block * tile, (block + 1) * tile)
+        n_one = (normed_ref[at, :] * gain + bias).astype(BF16)
         n_ref[at, :] = n_one
         out = mul(n_one, weight_ref[...])
         scale = jnp.where(iota(out.shape, 1) < part, HEAD_DIM ** (-0.5), 1.0)
@@ -218,8 +227,19 @@
         put[...] = att_wide_ref[at, :].astype(BF16)
 
 
+def unpack_body(shard_ref, mine_ref, other_ref, spread_ref, lines_ref, weight_ref, place_ref):
+    first_core = shard_ref[0, 0] % 2 == 0
+    half = mine_ref.shape[1]
+    left = jnp.where(first_core, mine_ref[...], other_ref[...])
+    right = jnp.where(first_core, other_ref[...], mine_ref[...])
+    weight_ref[:, :half] = mul(spread_ref[...], left).astype(BF16)
+    weight_ref[:, half:] = mul(spread_ref[...], right).astype(BF16)
+    slot = iota(place_ref.shape[1:], 0)
+    for k in range(2):
+        place_ref[k] = (slot == lines_ref[k : k + 1, :]).astype(F32).astype(BF16)
+
+
 def router_body(
-    held,
     n_dp,
     shard_ref,
     x_ref,
@@ -228,27 +248,19 @@
     sib_ref,
     far_ref,
     last_ref,
-    mine_ref,
-    other_ref,
+    weight_ref,
     gates_ref,
     vector_ref,
     routes_ref,
-    lines_ref,
-    weight_ref,
+    place_ref,
     resid_ref,
     x_two_ref,
     comb_ref,
     out_ref,
 ):
     rows, width = x_ref.shape
-    slots = out_ref.shape[0]
     part = near_ref.shape[1]
     shard = shard_ref[0, 0]
-    first_core = shard % 2 == 0
-    left = jnp.where(first_core, mine_ref[...], other_ref[...])
-    right = jnp.where(first_core, other_ref[...], mine_ref[...])
-    got = jnp.concatenate([left, right], 1)
-    weight_ref[...] = mul(spread(held, width, True), got).astype(BF16)
     gain, bias = vector_ref[2:3, :], vector_ref[3:4, :]
     resid = x_ref[...].astype(F32)
     for k, ref in enumerate((near_ref, sib_ref, far_ref.at[:rows], last_ref.at[rows:])):
@@ -268,9 +280,8 @@
     raw = [jnp.exp(c - top) for c in chosen]
     comb = [r / (raw[0] + raw[1]) for r in raw]
     comb_ref[...] = in_lanes(comb, rows)
-    slot = iota((slots, rows), 0)
-    place = [(slot == lines_ref[k : k + 1, :]).astype(F32).astype(BF16) for k in range(2)]
-    both = (place[0].astype(F32) + place[1].astype(F32)).astype(BF16)
+    place = [place_ref[k] for k in range(2)]
+    both = place[0] + place[1]
     out_ref[:, :width] = mul(both, x_two).astype(BF16)
     terms = [in_lanes(in_three(c), rows).astype(BF16) for c in comb]
     placed = mul(place[0], terms[0]) + mul(place[1], terms[1])
@@ -283,9 +294,9 @@
     rows_ref,
     *refs,
 ):
-    own_refs, sib_refs, far_ref = refs[:2], refs[2:4], refs[4]
-    back_ref, grad_y_ref, hidden_ref, grad_pre_ref = refs[5:9]
-    held_ref, hid_ref, pre_ref, sum_out_ref, sum_back_ref, sems, out_sems = refs[9:]
+    own_refs, sib_refs, far_refs = refs[:2], refs[2:4], refs[4:6]
+    back_ref, grad_y_ref, hidden_ref, grad_pre_ref = refs[6:10]
+    held_ref, hid_ref, pre_ref, sum_out_ref, sum_back_ref, sems, out_sems = refs[10:]
     slots, width = grad_y_ref.shape
     wide = width + 128
     chunk = 256
@@ -293,9 +304,9 @@
     shard = shard_ref[0, 0]
     sources = (
         own_refs,
-        [far_ref.at[shard ^ 2, k] for k in range(2)],
+        [ref.at[shard ^ 2] for ref in far_refs],
         sib_refs,
-        [far_ref.at[shard ^ 3, k] for k in range(2)],
+        [ref.at[shard ^ 3] for ref in far_refs],
     )
     copies = [
         [
@@ -407,37 +418,46 @@
         mul(rows_t_ref[...], grad_pre_ref[...]),
         mul(grad_y_t_ref[...], hidden_ref[...]),
     ]
-    for k, ref in enumerate(refs[-2:]):
-        grad = grads[k] if len(refs) == 2 else grads[k] + refs[k][...].astype(F32)
+    if len(refs) > 2:
+        grads = [grad + ref[...].astype(F32) for grad, ref in zip(grads, refs)]
+    if len(refs) == 3:
+        refs[2][0], refs[2][1] = (grad.astype(BF16) for grad in grads)
+        return
+    for grad, ref in zip(grads, refs[-2:]):
         ref[...] = grad.astype(ref.dtype)
 
 
-def weight_grads(rows_t, grad_y_t, hidden, grad_pre, which, dtype, sibs=()):
+def weight_grads(rows_t, grad_y_t, hidden, grad_pre, which, dtype, sibs=(), stacked=False):
     width, slots = grad_y_t.shape
     quarter = hidden.shape[1] // 4
     chunk = 256
     pieces = quarter // chunk
     whole = pl.BlockSpec((width, slots), lambda c: (0, 0))
     piece = pl.BlockSpec((slots, chunk), lambda c: (0, which * pieces + c))
+    shapes = (shaped((width, quarter), dtype),) * 2
+    out_specs = [pl.BlockSpec((width, chunk), lambda c: (0, c))] * 2
+    if stacked:
+        shapes = shaped((2, width, quarter), dtype)
+        out_specs = pl.BlockSpec((2, width, chunk), lambda c: (0, 0, c))
     return call(
         weight_grad_body,
-        (shaped((width, quarter), dtype),) * 2,
+        shapes,
         (rows_t, grad_y_t, hidden, grad_pre, *sibs),
         grid=(pieces,),
         in_specs=[whole] * 2
         + [piece] * 2
         + [pl.BlockSpec((width, chunk), lambda c: (0, c))] * len(sibs),
-        out_specs=[pl.BlockSpec((width, chunk), lambda c: (0, c))] * 2,
-    )
-
-
-def new_grads_body(shard_ref, in_ref, out_ref, far_in_ref, far_out_ref, grad_in_ref, grad_out_ref):
+        out_specs=out_specs,
+    )
+
+
+def new_grads_body(shard_ref, in_ref, out_ref, far_ref, grad_in_ref, grad_out_ref):
     new_here = shard_ref[0, 0] < 2
-    grad_in_ref[0] = jnp.where(new_here, in_ref[...], far_in_ref[0].astype(F32))
-    grad_out_ref[0] = jnp.where(new_here, out_ref[...], far_out_ref[0].astype(F32)).T
-
-
-def new_grads_call(shard, own, far_in, far_out):
+    grad_in_ref[0] = jnp.where(new_here, in_ref[...], far_ref[0, 0].astype(F32))
+    grad_out_ref[0] = jnp.where(new_here, out_ref[...], far_ref[0, 1].astype(F32)).T
+
+
+def new_grads_call(shard, own, far):
     quarter = own[0].shape[0]
     tile = quarter // 3
     piece = pl.BlockSpec((quarter, tile), lambda c: (0, c))
@@ -445,15 +465,15 @@
     return call(
         new_grads_body,
         (shaped((1, quarter, quarter), F32),) * 2,
-        (shard, *own, far_in, far_out),
+        (shard, *own, far),
         grid=(3,),
-        in_specs=[pl.BlockSpec(memory_space=SMEM), piece, piece, one, one],
+        in_specs=[pl.BlockSpec(memory_space=SMEM), piece, piece]
+        + [pl.BlockSpec((1, 2, quarter, tile), lambda c: (0, 0, 0, c))],
         out_specs=[one, pl.BlockSpec((1, tile, quarter), lambda c: (0, c, 0))],
     )
 
 
 def token_back_body(
-    held,
     n_dp,
     back_ref,
     cols_ref,
@@ -461,12 +481,12 @@
     comb_ref,
     grad_ref,
     resid_ref,
-    x_two_ref,
     gates_ref,
     vector_ref,
     resid_grad_ref,
     att_ref,
-    gate_ref,
+    dlogits_ref,
+    sums_ref,
 ):
     rows, width = grad_ref.shape
     slots = back_ref.shape[0]
@@ -493,11 +513,9 @@
     grad_resid = grad_ref[...].astype(F32) + norm_back(grad_x_two * gain, normed, scaling)
     resid_grad_ref[...] = grad_resid
     att_ref[...] = grad_resid.astype(BF16)
-    spread_all = spread(held, width, False)
-    turned = contract_cols(spread_all, x_two_ref[...]).astype(BF16)
-    own_gates = jnp.where(lane < n_dp, dlogits.astype(F32), 0.0).astype(BF16)
-    last = 128 - 2 * n_dp + n_dp
-    gate_ref[...] = mul(turned, own_gates) + sums_in_lanes(spread_all, sums, last)
+    dlogits_ref[...] = dlogits
+    sub = iota(sums_ref.shape, 0)
+    sums_ref[...] = jnp.where(sub == 0, sums[0], sums[1])
 
 
 def sums_in_lanes(spread_all, sums, first):
@@ -571,9 +589,9 @@
     grad_ref,
     *refs,
 ):
-    x_refs, owned_ref, part_refs = refs[:4], refs[4], refs[5:9]
-    grads_ref, key_ref, value_ref = refs[9:]
-    tile, width = x_refs[0].shape
+    normed_ref, owned_ref, part_refs = refs[0], refs[1], refs[2:6]
+    grads_ref, key_ref, value_ref = refs[6:]
+    tile, width = normed_ref.shape[0] // 4, normed_ref.shape[1]
     part = att_ref.shape[1]
     shard = shard_ref[0, 0]
     key_ref[...] = jnp.zeros_like(key_ref)
@@ -607,12 +625,11 @@
     grads_ref[:, part : 2 * part] = key_ref[...].astype(BF16)
     grads_ref[:, 2 * part :] = value_ref[...].astype(BF16)
     sums = [jnp.zeros((1, width), F32)] * 2
-    for k, (x_ref, part_ref) in enumerate(zip(x_refs, part_refs)):
+    for k, part_ref in enumerate(part_refs):
         at = pl.ds(pl.multiple_of((shard ^ k) * tile, tile), tile)
         grad_n = contract_cols(grads_ref[at, :], weight_ref[:, : 3 * part])
         part_ref[...] = grad_n.astype(BF16)
-        normed, unused = norm_stats(x_ref[...].astype(F32))
-        sums[0] += jnp.sum(grad_n * normed, 0, keepdims=True)
+        sums[0] += jnp.sum(grad_n * normed_ref[at, :], 0, keepdims=True)
         sums[1] += jnp.sum(grad_n, 0, keepdims=True)
     spread_all = spread(held, width, False)
     wide = 3 * part
@@ -659,13 +676,32 @@
         sums_ref[k : k + 1, :] = line[:, :held]
 
 
-def layer_out_body(rows_ref, cols_ref, comb_ref, resid_ref, out_ref):
+def layer_out_body(
+    held,
+    n_dp,
+    rows_ref,
+    cols_ref,
+    comb_ref,
+    resid_ref,
+    x_two_ref,
+    dlogits_ref,
+    sums_ref,
+    out_ref,
+    gate_ref,
+):
     slot = iota((cols_ref.shape[0], rows_ref.shape[0]), 1)
     out = resid_ref[...]
     for k in range(2):
         place = (slot == cols_ref[:, k : k + 1]).astype(F32).astype(BF16)
         out = out + comb_ref[:, k : k + 1] * mul(place, rows_ref[:, -out.shape[1] :])
     out_ref[...] = out.astype(BF16)
+    spread_all = spread(held, out.shape[1], False)
+    turned = contract_cols(spread_all, x_two_ref[...]).astype(BF16)
+    dlogits = dlogits_ref[...].astype(F32)
+    lane = iota(dlogits.shape, 1) - (128 - 2 * n_dp)
+    own_gates = jnp.where(lane < n_dp, dlogits, 0.0).astype(BF16)
+    sums = [sums_ref[0:1, :], sums_ref[1:2, :]]
+    gate_ref[...] = mul(turned, own_gates) + sums_in_lanes(spread_all, sums, 128 - n_dp)
 
 
 def per_device(
@@ -721,7 +757,9 @@
         return [pieces[0]] + [send(piece, k) for k, piece in enumerate(pieces) if k > 0]
 
     x_far, x_sib = send(tokens, 2), send(tokens, 1)
-    x_sib, query_weight = tie((x_sib, query_weight))
+    x_sib, new_in, new_out, frozen_in, frozen_out, query_weight = tie(
+        (x_sib, new_in, new_out, frozen_in, frozen_out, query_weight)
+    )
 
     half = width // 2
     wide = width + 128
@@ -736,26 +774,27 @@
         ),
         scratch_shapes=[pltpu.VMEM((n_shard, PAD, in_wide + half), F32)],
     )
-    blocks, x_far = tie((blocks, x_far))
-    weights = swap(blocks.reshape(n_all, PAD, in_wide + half))
-    x_last = send(x_far, 1)
-    x_last, new_in, new_out, frozen_in, frozen_out = tie(
-        (x_last, new_in, new_out, frozen_in, frozen_out)
-    )
-    x_parts = (tokens, x_sib, x_far, x_last)
-
     fresh, old = (new_in[0], new_out[0]), (frozen_in[0], frozen_out[0])
     own = [jnp.where(new_here, f, o) for f, o in zip(fresh, old)]
-    away = jnp.stack([jnp.where(new_here, o, f) for f, o in zip(fresh, old)])
+    away = [jnp.where(new_here, o, f) for f, o in zip(fresh, old)]
+    blocks, x_far, own, away = tie((blocks, x_far, own, away))
+    weights = swap(blocks.reshape(n_all, PAD, in_wide + half))
+    far = [lax.all_gather(array, "shard") for array in away]
     sib_own = [send(array, 1) for array in own]
+    x_parts = (tokens, x_sib, x_far, send(x_far, 1))
 
     cols, lines = call(
         functools.partial(slots_body, n_dp, capacity),
         (shaped((rows, 128), I32), shaped((8, rows), I32)),
         (routes, routes.T),
     )
-    weights, x_parts, sib_own, lines, away = tie((weights, x_parts, sib_own, lines, away))
-    far = lax.all_gather(away, "shard")
+    normed_one, spread_all = call(
+        functools.partial(prepare_body, held),
+        (shaped((group_len, width), F32), shaped((width, padded), BF16)),
+        (place, *x_parts),
+        in_specs=[spec_smem] + [spec_vmem] * 4,
+    )
+    weights, normed_one, sib_own, lines = tie((weights, normed_one, sib_own, lines))
     in_got = weights[:, :, :in_wide].reshape(padded, in_wide)
     out_mine = weights[:, :, in_wide:].reshape(padded, half)
 
@@ -771,34 +810,40 @@
             shaped((group_len, part), F32),
             shaped((8, group_len), F32),
         ),
-        (bounds, place, in_got, *x_parts),
-        in_specs=[spec_smem] * 2 + [spec_vmem] * 5,
+        (bounds, place, in_got, normed_one, spread_all),
+        in_specs=[spec_smem] * 2 + [spec_vmem] * 3,
     )
     out_sib = send(out_mine, 1)
     att_near, att_sib, att_far = att
     att_sib = send(att_sib, 1)
     att_sib, att_far = tie((att_sib, att_far))
     att_far = send(att_far, 2)
+    w_out, place_map = call(
+        unpack_body,
+        (shaped((width, width), BF16), shaped((2, slots, rows), BF16)),
+        (place, out_mine, out_sib, spread_all, lines),
+        in_specs=[spec_smem] + [spec_vmem] * 4,
+    )
+    att_far, w_out = tie((att_far, w_out))
     att = att_near, att_sib, att_far, send(att_far, 1)
 
-    w_out, resid, x_two, comb, buffer = call(
-        functools.partial(router_body, held, n_dp),
+    resid, x_two, comb, buffer = call(
+        functools.partial(router_body, n_dp),
         (
-            shaped((width, width), BF16),
             shaped((rows, width), F32),
             shaped((rows, width), BF16),
             shaped((rows, 128), F32),
             shaped((slots, wide + width), BF16),
         ),
         (
-            *(place, tokens, cotangent, *att, out_mine, out_sib),
-            *(w_in, vectors, routes, lines),
+            *(place, tokens, cotangent, *att, w_out),
+            *(w_in, vectors, routes, place_map),
         ),
-        in_specs=[spec_smem] + [spec_vmem] * 12,
+        in_specs=[spec_smem] + [spec_vmem] * 11,
     )
     got = dispatch(buffer)
 
-    back, grad_y, hidden, grad_pre = expert_call(place, got, (*own, *sib_own, far))
+    back, grad_y, hidden, grad_pre = expert_call(place, got, (*own, *sib_own, *far))
     back_got = dispatch(back)
 
     rows_t, grad_y_t = call(turn_body, (shaped((width, slots), BF16),) * 2, (got, grad_y))
@@ -808,26 +853,30 @@
     sent_own = weight_grads(rows_t, grad_y_t, hidden, grad_pre, 2, BF16)
     rows_t, sent_own = tie((rows_t, sent_own))
     sibs_own = [send(array, 1) for array in sent_own]
-    away_in, away_out = weight_grads(rows_t, grad_y_t, hidden, grad_pre, 1, BF16, sibs)
-    far_in, far_out = (
-        lax.all_gather(array, "shard", axis_index_groups=pairs) for array in (away_in, away_out)
-    )
-    own_new = weight_grads(rows_t, grad_y_t, hidden, grad_pre, 0, F32, sibs_own)
-    back_got, own_new = tie((back_got, own_new))
-
-    resid_grad, att_grad, gate_part = call(
-        functools.partial(token_back_body, held, n_dp),
-        (shaped((rows, width), F32), shaped((rows, width), BF16), shaped((padded, 128), F32)),
-        (back_got, cols, routes, comb, cotangent, resid, x_two, w_in, vectors),
+    away_sum = weight_grads(rows_t, grad_y_t, hidden, grad_pre, 1, BF16, sibs, True)
+    far_sum = lax.all_gather(away_sum, "shard", axis_index_groups=pairs)
+    back_got, rows_t = tie((back_got, rows_t))
+
+    resid_grad, att_grad, dlogits, ln_two_sums = call(
+        functools.partial(token_back_body, n_dp),
+        (
+            shaped((rows, width), F32),
+            shaped((rows, width), BF16),
+            shaped((rows, 128), BF16),
+            shaped((8, width), F32),
+        ),
+        (back_got, cols, routes, comb, cotangent, resid, w_in, vectors),
     )
     grad_far = send(att_grad, 2)
     grad_sib = send(att_grad, 1)
-    layer_out = call(
-        layer_out_body,
-        shaped((rows, width), BF16),
-        (back_got, cols, comb, resid),
-    )
-    grad_far, layer_out = tie((grad_far, layer_out))
+    rows_t, grad_sib = tie((rows_t, grad_sib))
+    own_new = weight_grads(rows_t, grad_y_t, hidden, grad_pre, 0, F32, sibs_own)
+    layer_out, gate_part = call(
+        functools.partial(layer_out_body, held, n_dp),
+        (shaped((rows, width), BF16), shaped((padded, 128), F32)),
+        (back_got, cols, comb, resid, x_two, dlogits, ln_two_sums),
+    )
+    grad_far, layer_out, own_new = tie((grad_far, layer_out, own_new))
     grad_last = send(grad_far, 1)
     extent = padded // n_shard
     head_grad, *out_pieces = call(
@@ -844,8 +893,11 @@
     second_owned, *norm_part = call(
         functools.partial(attention_back_body, held),
         (shaped((padded, last_wide), BF16), *[shaped((rows, width), BF16)] * n_shard),
-        (bounds, place, n_one, qkv, att_wide, log_total, w_in, gate_part, head_grad, *x_parts),
-        in_specs=[spec_smem] * 2 + [spec_vmem] * 11,
+        (
+            *(bounds, place, n_one, qkv, att_wide, log_total, w_in, gate_part, head_grad),
+            normed_one,
+        ),
+        in_specs=[spec_smem] * 2 + [spec_vmem] * 8,
         scratch_shapes=[
             pltpu.VMEM((group_len, 3 * part), BF16),
             pltpu.VMEM((group_len, part), F32),
@@ -866,7 +918,7 @@
         input_output_aliases={1: 0},
     )
     second_got = swap(second_owned.reshape(n_all, PAD, last_wide)).reshape(padded, last_wide)
-    grads_new = new_grads_call(place, own_new, far_in, far_out)
+    grads_new = new_grads_call(place, own_new, far_sum)
     norm_far, grads_new = tie((norm_far, grads_new))
     grad_tokens = call(
         first_norm_back_body,

time: 376 us -> 375 us (level)
  waiting for transfers between devices: 90.7 us -> 73.7 us
  blocking collectives: 56.3 us -> 73.2 us
  Pallas kernels: 136 us -> 146 us
  starting transfers between devices: 53.5 us -> 45.7 us
  other arithmetic: 7.85 us -> 4.02 us
    all_gather x3, waiting for transfers between devices: 23.2 us -> 0.01 us  [the longest x2 0.01 us: per_device(): far = [lax.all_gather(array, 'shard') for array in away]]
    all_to_all x1, blocking collectives: 56.3 us -> 73.2 us  [swap(): lax.all_to_all(array, BOTH, split_axis=0, concat_axis=0, tiled=True, axis...]
    all_to_all x3, waiting for transfers between devices: 17.5 us -> 33.3 us  [swap(): lax.all_to_all(array, BOTH, split_axis=0, concat_axis=0, tiled=True, axis...]
    ppermute x22, waiting for transfers between devices: 49.9 us -> 39.6 us  [send(): return lax.ppermute(array, 'shard', [(k, k ^ step) for k in range(n_shard)])]
    pallas_call x18 -> x20, Pallas kernels: 136 us -> 146 us  [call(): pl.pallas_call(body, out_shape=out_shapes, compiler_params=pltpu.Compiler...]
    all_to_all x3, starting transfers between devices: 27.1 us -> 22.6 us  [swap(): lax.all_to_all(array, BOTH, split_axis=0, concat_axis=0, tiled=True, axis...]
    unnamed x57 -> x51, local copies, waits for them, and re-layouts: 10.2 us -> 10.5 us
  transfers between devices with their start and end apart: 28 -> 28, of which waited for: 13 -> 11; matrix products, arithmetic and copies ran while one was open for 3% -> 2% of each run, Pallas kernels for 28% -> 31%
where the time goes in v2:
time: 375 us; the launch traced here: 370 us
  Pallas kernels  146 us (39%)
  waiting for transfers between devices  73.7 us (20%)
  blocking collectives  73.2 us (20%)
  starting transfers between devices  45.7 us (12%)
  between operations  14.4 us (4%)
  local copies, waits for them, and re-layouts  13.2 us (4%)
  other arithmetic  4.02 us (1%)
    pallas_call x20, Pallas kernels, call(): pl.pallas_call(body, out_shape=out_shapes, compiler_params=pltpu.Compiler...  146 us
    all_to_all x1, blocking collectives, swap(): lax.all_to_all(array, BOTH, split_axis=0, concat_axis=0, tiled=True, axis...  73.2 us
    ppermute x22, waiting for transfers between devices, send(): return lax.ppermute(array, 'shard', [(k, k ^ step) for k in range(n_shard)])  39.6 us
    all_to_all x3, waiting for transfers between devices, swap(): lax.all_to_all(array, BOTH, split_axis=0, concat_axis=0, tiled=True, axis...  33.3 us
    ppermute x22, starting transfers between devices, send(): return lax.ppermute(array, 'shard', [(k, k ^ step) for k in range(n_shard)])  23 us
    all_to_all x3, starting transfers between devices, swap(): lax.all_to_all(array, BOTH, split_axis=0, concat_axis=0, tiled=True, axis...  22.6 us
    unnamed x51, local copies, waits for them, and re-layouts  10.5 us
  transfers between devices with their start and end apart: 28, of which 11 were waited for; matrix products, arithmetic and copies ran while one was open for 2% of the time, Pallas kernels for 31%

profile of v2, /device:TPU:1, one launch (start us, length us, event | category | flops | bytes accessed | tf_op | source)
XLA Modules:
  0.0 369.7 jit_solution(10091366803575381871)
XLA Ops:
  8.7 3.0 collective-permute-start.1
  12.5 2.4 shard_map.273
  14.9 3.9 %select_bitcast_fusion = (bf16[768,768]{1,0:T(8,128)(2,1)}, bf16[768,768]{1,0:T(8,128)(2,1)S(1)}, bf16[768,768]{1,0:T(8,128)(2,1)}, bf16[768,768]{1,0:T(8,128)(2,1)}) fusion(bf16[1,768,768]{2,1,0:T(8,128)(2,1)S(1)} %copy-done.4, bf16[1,768,768]{2,1,0:T(8,128)(2,1)} %param.32, pred[]{:T(512)S(6)} %lt.3, bf16[1,768,768]{2,1,0:T(8,128)(2,1)} %param.31, ...), kind=kLoop, calls=%fused_computation.1 | loop fusion | flops 2359296 | bytes 9437185 | tf_op jit(solution)/shard_map/jit(_where)/select_n | solution.py:779
  18.8 2.3 collective-permute-done.1.refs_2_
  22.0 10.9 %all-to-all-start = ((bf16[128,8,1024]{2,1,0:T(8,128)(2,1)}), bf16[128,8,1024]{2,1,0:T(8,128)(2,1)S(1)}, u32[]{:S(2)}, u32[]{:S(2)}) async-start(bf16[128,8,1024]{2,1,0:T(8,128)(2,1)} %bitcast.40), calls=%async_computation | async-start | bytes 4194304 | tf_op jit(solution)/shard_map/all_to_all | solution.py:746
  39.2 4.4 %shard_map.274 = (f32[1024,768]{1,0:T(8,128)}, bf16[768,1024]{1,0:T(8,128)(2,1)}) custom-call(s32[1,1]{1,0:T(1,128)} %bitcast.shard_ref, bf16[256,768]{1,0:T(8,128)(2,1)} %x_ref.3, bf16[256,768]{1,0:T(8,128)(2,1)} %copy-done.11, bf16[256,768]{1,0:T(8,128)(2,1)} %copy-done.12, bf16[256,768]{1,0:T(8,128)(2,1)} %collective-permute-done.2.refs_3_), custom_call_target="tpu_custom_call" | custom-call | flops 1 | bytes 1 | tf_op jit(solution)/shard_map/pallas_call | solution.py:88
  43.6 20.6 %all-to-all-done = bf16[128,8,1024]{2,1,0:T(8,128)(2,1)S(1)} async-done(((bf16[128,8,1024]{2,1,0:T(8,128)(2,1)}), bf16[128,8,1024]{2,1,0:T(8,128)(2,1)S(1)}, u32[]{:S(2)}, u32[]{:S(2)}) %all-to-all-start) | async-done | bytes 2097184 | tf_op jit(solution)/shard_map/all_to_all | solution.py:746
  67.8 13.8 %shard_map.276 = (bf16[768,640]{1,0:T(8,128)(2,1)}, f32[8,768]{1,0:T(8,128)}, bf16[1024,768]{1,0:T(8,128)(2,1)}, bf16[1024,640]{1,0:T(8,128)(2,1)}, bf16[256,192...) custom-call(s32[1,2]{1,0:T(1,128)} %bounds_ref.3, ...), custom_call_target="tpu_custom_call" | custom-call | flops 1 | bytes 1 | tf_op jit(solution)/shard_map/pallas_call | solution.py:88
  84.1 5.1 %shard_map.277 = (bf16[768,768]{1,0:T(8,128)(2,1)}, bf16[2,1024,256]{2,1,0:T(8,128)(2,1)}) custom-call(s32[1,1]{1,0:T(1,128)} %bitcast.shard_ref, bf16[1024,384]{1,0:T(8,128)(2,1)} %copy-done.3, bf16[1024,384]{1,0:T(8,128)(2,1)} %copy-done.7, bf16[768,1024]{1,0:T(8,128)(2,1)} %get-tuple-element.120.spread_ref, s32[8,256]{1,0:T(8,128)} %get-tuple-element.126.lines_ref), custom_call_target="tpu_custom_call" | custom-call | flops 1 | bytes 1 | tf_op jit(solution)/shard_map/pallas_call | solution.py:88
  89.3 3.4 collective-permute-done.6.far_ref
  95.5 7.1 %shard_map.278 = (f32[256,768]{1,0:T(8,128)}, bf16[256,768]{1,0:T(8,128)(2,1)}, f32[256,128]{1,0:T(8,128)}, bf16[1024,1664]{1,0:T(8,128)(2,1)}) custom-call(s32[1,1]{1,0:T(1,128)} %bitcast.shard_ref, bf16[256,768]{1,0:T(8,128)(2,1)} %x_ref.3, bf16[256,768]{1,0:T(8,128)(2,1)} %grad_ref.3, bf16[256,192]{1,0:T(8,128)(2,1)} %get-tuple-element.121.near_ref, ...), custom_call_target="tpu_custom_call" | custom-call | flops 1 | bytes 1 | tf_op jit(solution)/shard_map/pallas_call | solution.py:88
  102.6 73.2 %all_to_all.20 = bf16[64,16,1664]{2,1,0:T(8,128)(2,1)} all-to-all(bf16[64,16,1664]{2,1,0:T(8,128)(2,1)} %bitcast.47), channel_id=1, replica_groups={{0,2,4,6,8,10,12,14,16,18,20,22,24,26,28,30,32,34,36,38,40,42,44,46,48,..., dimensions={0} | all-to-all | bytes 6815744 | tf_op jit(solution)/shard_map/all_to_all | solution.py:746
  175.8 29.8 %shard_map.279 = (bf16[1024,1664]{1,0:T(8,128)(2,1)}, bf16[1024,768]{1,0:T(8,128)(2,1)}, bf16[1024,3072]{1,0:T(8,128)(2,1)}, bf16[1024,3072]{1,0:T(8,128)(2,1)}) custom-call(s32[1,1]{1,0:T(1,128)} %bitcast.shard_ref, bf16[1024,1664]{1,0:T(8,128)(2,1)} %bitcast.36, bf16[768,768]{1,0:T(8,128)(2,1)} %get-tuple-element.115.refs_0_, bf16[768,768]{1,0:T(8,128)(2,1)} %copy-done.2, ...), custom_call_target="tpu_custom_call" | custom-call | flops 1 | bytes 1 | tf_op jit(solution)/shard_map/pallas_call | solution.py:88
  205.6 5.8 %all-to-all-start.2 = ((bf16[64,16,1664]{2,1,0:T(8,128)(2,1)}), bf16[64,16,1664]{2,1,0:T(8,128)(2,1)S(1)}, u32[]{:S(2)}, u32[]{:S(2)}) async-start(bf16[64,16,1664]{2,1,0:T(8,128)(2,1)} %bitcast.46), calls=%async_computation.2 | async-start | bytes 6815744 | tf_op jit(solution)/shard_map/all_to_all | solution.py:746
  211.4 4.6 %shard_map.280 = (bf16[768,1024]{1,0:T(8,128)(2,1)}, bf16[768,1024]{1,0:T(8,128)(2,1)}) custom-call(bf16[1024,1664]{1,0:T(8,128)(2,1)} %bitcast.37, bf16[1024,768]{1,0:T(8,128)(2,1)} %get-tuple-element.139.grad_y_ref), custom_call_target="tpu_custom_call" | custom-call | flops 1 | bytes 1 | tf_op jit(solution)/shard_map/pallas_call | solution.py:88
  216.0 6.7 %shard_map.281 = (bf16[768,768]{1,0:T(8,128)(2,1)}, bf16[768,768]{1,0:T(8,128)(2,1)}) custom-call(bf16[768,1024]{1,0:T(8,128)(2,1)} %get-tuple-element.160.rows_t_ref, bf16[768,1024]{1,0:T(8,128)(2,1)} %get-tuple-element.141.grad_y_t_ref, bf16[1024,3072]{1,0:T(8,128)(2,1)} %get-tuple-element.142.hidden_ref, bf16[1024,3072]{1,0:T(8,128)(2,1)} %get-tuple-element.143.grad_pre_ref), custom_call_target="tpu_custom_call" | custom-call | flops 1 | bytes 1 | tf_op jit(solution)/shard_map/pallas_call | solution.py:88
  224.0 7.0 %shard_map.282 = (bf16[768,768]{1,0:T(8,128)(2,1)}, bf16[768,768]{1,0:T(8,128)(2,1)}) custom-call(bf16[768,1024]{1,0:T(8,128)(2,1)} %get-tuple-element.160.rows_t_ref, bf16[768,1024]{1,0:T(8,128)(2,1)} %get-tuple-element.141.grad_y_t_ref, bf16[1024,3072]{1,0:T(8,128)(2,1)} %get-tuple-element.142.hidden_ref, bf16[1024,3072]{1,0:T(8,128)(2,1)} %get-tuple-element.143.grad_pre_ref), custom_call_target="tpu_custom_call" | custom-call | flops 1 | bytes 1 | tf_op jit(solution)/shard_map/pallas_call | solution.py:88
  233.0 7.3 %shard_map.288 = bf16[2,768,768]{2,1,0:T(8,128)(2,1)} custom-call(bf16[768,1024]{1,0:T(8,128)(2,1)} %get-tuple-element.160.rows_t_ref, bf16[768,1024]{1,0:T(8,128)(2,1)} %get-tuple-element.141.grad_y_t_ref, bf16[1024,3072]{1,0:T(8,128)(2,1)} %get-tuple-element.142.hidden_ref, bf16[1024,3072]{1,0:T(8,128)(2,1)} %get-tuple-element.143.grad_pre_ref, ...), custom_call_target="tpu_custom_call" | custom-call | flops 1 | bytes 1 | tf_op jit(solution)/shard_map/pallas_call | solution.py:88
  240.9 12.7 %all-to-all-done.2 = bf16[64,16,1664]{2,1,0:T(8,128)(2,1)S(1)} async-done(((bf16[64,16,1664]{2,1,0:T(8,128)(2,1)}), bf16[64,16,1664]{2,1,0:T(8,128)(2,1)S(1)}, u32[]{:S(2)}, u32[]{:S(2)}) %all-to-all-start.2) | async-done | bytes 3407904 | tf_op jit(solution)/shard_map/all_to_all | solution.py:746
  255.3 6.6 %shard_map.283 = (f32[256,768]{1,0:T(8,128)}, bf16[256,768]{1,0:T(8,128)(2,1)}, bf16[256,128]{1,0:T(8,128)(2,1)}, f32[8,768]{1,0:T(8,128)}) custom-call(bf16[1024,1664]{1,0:T(8,128)(2,1)} %bitcast.38, s32[256,128]{1,0:T(8,128)} %get-tuple-element.151.cols_ref, s32[256,2]{1,0:T(8,128)} %copy.35.routes_ref, f32[256,128]{1,0:T(8,128)} %get-tuple-element.152.comb_ref, ...), custom_call_target="tpu_custom_call" | custom-call | flops 1 | bytes 1 | tf_op jit(solution)/shard_map/pallas_call | solution.py:88
  261.9 2.4 collective-permute-start.10
  264.9 5.3 %shard_map.284 = (bf16[256,768]{1,0:T(8,128)(2,1)}, f32[1024,128]{1,0:T(8,128)}) custom-call(bf16[1024,1664]{1,0:T(8,128)(2,1)} %bitcast.39, s32[256,128]{1,0:T(8,128)} %get-tuple-element.151.cols_ref, f32[256,128]{1,0:T(8,128)} %get-tuple-element.152.comb_ref, f32[256,768]{1,0:T(8,128)} %get-tuple-element.153.resid_ref, ...), custom_call_target="tpu_custom_call" | custom-call | flops 1 | bytes 1 | tf_op jit(solution)/shard_map/pallas_call | solution.py:88
  270.2 8.3 %shard_map.285 = (f32[768,768]{1,0:T(8,128)}, f32[768,768]{1,0:T(8,128)}) custom-call(bf16[768,1024]{1,0:T(8,128)(2,1)} %get-tuple-element.160.rows_t_ref, bf16[768,1024]{1,0:T(8,128)(2,1)} %get-tuple-element.141.grad_y_t_ref, bf16[1024,3072]{1,0:T(8,128)(2,1)} %get-tuple-element.142.hidden_ref, bf16[1024,3072]{1,0:T(8,128)(2,1)} %get-tuple-element.143.grad_pre_ref, ...), custom_call_target="tpu_custom_call" | custom-call | flops 1 | bytes 1 | tf_op jit(solution)/shard_map/pallas_call | solution.py:88
  278.5 7.0 %collective-permute-done.9.far_ref = bf16[256,768]{1,0:T(8,128)(2,1)S(1)} collective-permute-done((bf16[256,768]{1,0:T(8,128)(2,1)}, bf16[256,768]{1,0:T(8,128)(2,1)S(1)}, u32[]{:S(2)}, u32[]{:S(2)}) %collective-permute-start.9) | collective-permute-done | bytes 393248 | tf_op jit(solution)/shard_map/ppermute | solution.py:754
  288.4 4.1 %shard_map.286 = (bf16[1024,192]{1,0:T(8,128)(2,1)}, bf16[256,192]{1,0:T(8,128)(2,1)}, bf16[256,192]{1,0:T(8,128)(2,1)}, bf16[256,192]{1,0:T(8,128)(2,1)}, bf16[256,192]{1,0:T(8,128)(2,1)}) custom-call(s32[1,1]{1,0:T(1,128)} %bitcast.shard_ref, f32[1024,192]{1,0:T(8,128)} %get-tuple-element.168.att_ref, bf16[768,768]{1,0:T(8,128)(2,1)} %get-tuple-element.129.weight_ref, ...), custom_call_target="tpu_custom_call" | custom-call | flops 1 | bytes 1 | tf_op jit(solution)/shard_map/pallas_call | solution.py:88
  293.4 3.0 collective-permute-start.21
  296.4 17.4 %shard_map.287 = (bf16[1024,896]{1,0:T(8,128)(2,1)}, bf16[256,768]{1,0:T(8,128)(2,1)}, bf16[256,768]{1,0:T(8,128)(2,1)}, bf16[256,768]{1,0:T(8,128)(2,1)}, bf16[256,768]{1,0:T(8,128)(2,1)}) custom-call(s32[1,2]{1,0:T(1,128)} %bounds_ref.3, s32[1,1]{1,0:T(1,128)} %bitcast.shard_ref, bf16[1024,768]{1,0:T(8,128)(2,1)} %get-tuple-element.166.n_ref, ...), custom_call_target="tpu_custom_call" | custom-call | flops 1 | bytes 1 | tf_op jit(solution)/shard_map/pallas_call | solution.py:88
  316.6 5.9 %all-to-all-start.3 = ((bf16[128,8,896]{2,1,0:T(8,128)(2,1)}), bf16[128,8,896]{2,1,0:T(8,128)(2,1)S(1)}, u32[]{:S(2)}, u32[]{:S(2)}) async-start(bf16[128,8,896]{2,1,0:T(8,128)(2,1)} %bitcast.42), calls=%async_computation.3 | async-start | bytes 3670016 | tf_op jit(solution)/shard_map/all_to_all | solution.py:746
  328.0 6.2 %shard_map.289 = (f32[1,768,768]{2,1,0:T(8,128)}, f32[1,768,768]{2,1,0:T(8,128)}) custom-call(s32[1,1]{1,0:T(1,128)} %bitcast.shard_ref, f32[768,768]{1,0:T(8,128)} %get-tuple-element.178.in_ref, f32[768,768]{1,0:T(8,128)} %get-tuple-element.179.out_ref, bf16[2,2,768,768]{3,2,1,0:T(8,128)(2,1)} %bitcast.45), custom_call_target="tpu_custom_call" | custom-call | flops 1 | bytes 1 | tf_op jit(solution)/shard_map/pallas_call | solution.py:88
  334.2 19.6 %collective-permute-done.16.far_ref = bf16[256,768]{1,0:T(8,128)(2,1)S(1)} collective-permute-done((bf16[256,768]{1,0:T(8,128)(2,1)S(1)}, bf16[256,768]{1,0:T(8,128)(2,1)S(1)}, u32[]{:S(2)}, u32[]{:S(2)}) %collective-permute-start.16) | collective-permute-done | bytes 393248 | tf_op jit(solution)/shard_map/ppermute | solution.py:754
  354.7 3.0 shard_map.290
  359.0 2.5 shard_map.292
  (104 shorter events, 40.0 us)
Async XLA Ops:
  7.2 168.6 %all-gather.7.cloned.1.call-start = ((), (), s32[]{:S(2)}) async-start(), calls=%async_computation.4 | async-start | bytes 5898240 | tf_op jit(solution)/shard_map/all_gather | solution.py:782
  7.2 4.5 %collective-permute-start = (bf16[256,768]{1,0:T(8,128)(2,1)}, bf16[256,768]{1,0:T(8,128)(2,1)S(1)}, u32[]{:S(2)}, u32[]{:S(2)}) collective-permute-start(bf16[256,768]{1,0:T(8,128)(2,1)} %x_ref.3), channel_id=1, source_target_pairs={{0,1},{1,0},{2,3},{3,2},{4,5},{5,4},{6,7},{7,6},{8,9},{9,8},{10,11... | collective-permute-start | bytes 1179656 | tf_op jit(solution)/shard_map/ppermute | solution.py:754
  8.7 12.4 %collective-permute-start.1 = (bf16[256,768]{1,0:T(8,128)(2,1)}, bf16[256,768]{1,0:T(8,128)(2,1)S(1)}, u32[]{:S(2)}, u32[]{:S(2)}) collective-permute-start(bf16[256,768]{1,0:T(8,128)(2,1)} %x_ref.3), channel_id=1, source_target_pairs={{0,2},{1,3},{2,0},{3,1},{4,6},{5,7},{6,4},{7,5},{8,10},{9,11},{10,... | collective-permute-start | bytes 1179656 | tf_op jit(solution)/shard_map/ppermute | solution.py:754
  18.8 15.2 %copy-start.2 = (bf16[768,768]{1,0:T(8,128)(2,1)}, bf16[768,768]{1,0:T(8,128)(2,1)S(1)}, u32[]{:S(2)}) copy-start(bf16[768,768]{1,0:T(8,128)(2,1)S(1)} %get-tuple-element.116.refs_1_) | copy-start | bytes 3538948
  21.2 154.6 %all-gather.9.cloned.1.call-start = ((), (), s32[]{:S(2)}) async-start(), calls=%async_computation.5 | async-start | bytes 5898240 | tf_op jit(solution)/shard_map/all_gather | solution.py:782
  21.9 12.6 %copy-start.22 = (s32[256,2]{0,1:T(2,128)S(1)}, s32[256,2]{0,1:T(2,128)}, u32[]{:S(2)}) copy-start(s32[256,2]{0,1:T(2,128)} %param.20) | copy-start | bytes 6148
  22.0 42.3 %all-to-all-start = ((bf16[128,8,1024]{2,1,0:T(8,128)(2,1)}), bf16[128,8,1024]{2,1,0:T(8,128)(2,1)S(1)}, u32[]{:S(2)}, u32[]{:S(2)}) async-start(bf16[128,8,1024]{2,1,0:T(8,128)(2,1)} %bitcast.40), calls=%async_computation | async-start | bytes 4194304 | tf_op jit(solution)/shard_map/all_to_all | solution.py:746
  32.9 10.7 %collective-permute-start.3 = (bf16[768,768]{1,0:T(8,128)(2,1)}, bf16[768,768]{1,0:T(8,128)(2,1)}, u32[]{:S(2)}, u32[]{:S(2)}) collective-permute-start(bf16[768,768]{1,0:T(8,128)(2,1)} %get-tuple-element.115.refs_0_), channel_id=1, source_target_pairs={{0,1},{1,0},{2,3},{3,2},{4,5},{5,4},{6,7},{7,6},{8,9},{9,8},{10,11... | collective-permute-start | bytes 3538952 | tf_op jit(solution)/shard_map/ppermute | solution.py:754
  34.0 9.6 %collective-permute-start.4 = (bf16[768,768]{1,0:T(8,128)(2,1)S(1)}, bf16[768,768]{1,0:T(8,128)(2,1)}, u32[]{:S(2)}, u32[]{:S(2)}) collective-permute-start(bf16[768,768]{1,0:T(8,128)(2,1)S(1)} %get-tuple-element.116.refs_1_), channel_id=1, source_target_pairs={{0,1},{1,0},{2,3},{3,2},{4,5},{5,4},{6,7},{7,6},{8,9},{9,8},{10,11... | collective-permute-start | bytes 3538952 | tf_op jit(solution)/shard_map/ppermute | solution.py:754
  34.1 5.0 %collective-permute-start.2 = (bf16[256,768]{1,0:T(8,128)(2,1)}, bf16[256,768]{1,0:T(8,128)(2,1)}, u32[]{:S(2)}, u32[]{:S(2)}) collective-permute-start(bf16[256,768]{1,0:T(8,128)(2,1)} %copy-done.12), channel_id=1, source_target_pairs={{0,1},{1,0},{2,3},{3,2},{4,5},{5,4},{6,7},{7,6},{8,9},{9,8},{10,11... | collective-permute-start | bytes 1179656 | tf_op jit(solution)/shard_map/ppermute | solution.py:754
  64.4 18.9 %collective-permute-start.7 = (bf16[1024,384]{1,0:T(8,128)(2,1)S(1)}, bf16[1024,384]{1,0:T(8,128)(2,1)S(1)}, u32[]{:S(2)}, u32[]{:S(2)}) collective-permute-start(bf16[1024,384]{1,0:T(8,128)(2,1)S(1)} %slice_bitcast_fusion.1.mine_ref), channel_id=1, source_target_pairs={{0,1},{1,0},{2,3},{3,2},{4,5},{5,4},{6,7},{7,6},{8,9},{9,8},{10,11... | collective-permute-start | bytes 2359304 | tf_op jit(solution)/shard_map/ppermute | solution.py:754
  81.5 1.6 collective-permute-start.5
  83.2 11.6 %copy-start.19 = (bf16[256,192]{1,0:T(8,128)(2,1)}, bf16[256,192]{1,0:T(8,128)(2,1)S(1)}, u32[]{:S(2)}) copy-start(bf16[256,192]{1,0:T(8,128)(2,1)S(1)} %collective-permute-done.5.sib_ref) | copy-start | bytes 294916
  83.2 9.5 %collective-permute-start.6 = (bf16[512,192]{1,0:T(8,128)(2,1)}, bf16[512,192]{1,0:T(8,128)(2,1)S(1)}, u32[]{:S(2)}, u32[]{:S(2)}) collective-permute-start(bf16[512,192]{1,0:T(8,128)(2,1)} %get-tuple-element.125), channel_id=1, source_target_pairs={{0,2},{1,3},{2,0},{3,1},{4,6},{5,7},{6,4},{7,5},{8,10},{9,11},{10,... | collective-permute-start | bytes 589832 | tf_op jit(solution)/shard_map/ppermute | solution.py:754
  92.7 2.1 collective-permute-start.8
  205.6 48.0 %all-to-all-start.2 = ((bf16[64,16,1664]{2,1,0:T(8,128)(2,1)}), bf16[64,16,1664]{2,1,0:T(8,128)(2,1)S(1)}, u32[]{:S(2)}, u32[]{:S(2)}) async-start(bf16[64,16,1664]{2,1,0:T(8,128)(2,1)} %bitcast.46), calls=%async_computation.2 | async-start | bytes 6815744 | tf_op jit(solution)/shard_map/all_to_all | solution.py:746
  211.4 116.6 %all-gather.11.cloned.1.call-start = ((), (), s32[]{:S(2)}) async-start(), calls=%async_computation.6 | async-start | bytes 7077888 | tf_op jit(solution)/shard_map/all_gather | solution.py:857
  222.8 8.2 %collective-permute-start.17 = (bf16[768,768]{1,0:T(8,128)(2,1)}, bf16[768,768]{1,0:T(8,128)(2,1)S(1)}, u32[]{:S(2)}, u32[]{:S(2)}) collective-permute-start(bf16[768,768]{1,0:T(8,128)(2,1)} %get-tuple-element.180), channel_id=1, source_target_pairs={{0,1},{1,0},{2,3},{3,2},{4,5},{5,4},{6,7},{7,6},{8,9},{9,8},{10,11... | collective-permute-start | bytes 3538952 | tf_op jit(solution)/shard_map/ppermute | solution.py:754
  223.9 7.1 %collective-permute-start.18 = (bf16[768,768]{1,0:T(8,128)(2,1)}, bf16[768,768]{1,0:T(8,128)(2,1)S(1)}, u32[]{:S(2)}, u32[]{:S(2)}) collective-permute-start(bf16[768,768]{1,0:T(8,128)(2,1)} %get-tuple-element.181), channel_id=1, source_target_pairs={{0,1},{1,0},{2,3},{3,2},{4,5},{5,4},{6,7},{7,6},{8,9},{9,8},{10,11... | collective-permute-start | bytes 3538952 | tf_op jit(solution)/shard_map/ppermute | solution.py:754
  240.3 29.9 %collective-permute-start.11 = (bf16[768,768]{1,0:T(8,128)(2,1)}, bf16[768,768]{1,0:T(8,128)(2,1)}, u32[]{:S(2)}, u32[]{:S(2)}) collective-permute-start(bf16[768,768]{1,0:T(8,128)(2,1)} %get-tuple-element.161), channel_id=1, source_target_pairs={{0,1},{1,0},{2,3},{3,2},{4,5},{5,4},{6,7},{7,6},{8,9},{9,8},{10,11... | collective-permute-start | bytes 3538952 | tf_op jit(solution)/shard_map/ppermute | solution.py:754
  240.8 29.4 %collective-permute-start.12 = (bf16[768,768]{1,0:T(8,128)(2,1)}, bf16[768,768]{1,0:T(8,128)(2,1)}, u32[]{:S(2)}, u32[]{:S(2)}) collective-permute-start(bf16[768,768]{1,0:T(8,128)(2,1)} %get-tuple-element.162), channel_id=1, source_target_pairs={{0,1},{1,0},{2,3},{3,2},{4,5},{5,4},{6,7},{7,6},{8,9},{9,8},{10,11... | collective-permute-start | bytes 3538952 | tf_op jit(solution)/shard_map/ppermute | solution.py:754
  261.9 8.2 %collective-permute-start.10 = (bf16[256,768]{1,0:T(8,128)(2,1)}, bf16[256,768]{1,0:T(8,128)(2,1)S(1)}, u32[]{:S(2)}, u32[]{:S(2)}) collective-permute-start(bf16[256,768]{1,0:T(8,128)(2,1)} %get-tuple-element.154.near_ref), channel_id=1, source_target_pairs={{0,1},{1,0},{2,3},{3,2},{4,5},{5,4},{6,7},{7,6},{8,9},{9,8},{10,11... | collective-permute-start | bytes 1179656 | tf_op jit(solution)/shard_map/ppermute | solution.py:754
  264.3 21.2 %collective-permute-start.9 = (bf16[256,768]{1,0:T(8,128)(2,1)}, bf16[256,768]{1,0:T(8,128)(2,1)S(1)}, u32[]{:S(2)}, u32[]{:S(2)}) collective-permute-start(bf16[256,768]{1,0:T(8,128)(2,1)} %get-tuple-element.154.near_ref), channel_id=1, source_target_pairs={{0,2},{1,3},{2,0},{3,1},{4,6},{5,7},{6,4},{7,5},{8,10},{9,11},{10,... | collective-permute-start | bytes 1179656 | tf_op jit(solution)/shard_map/ppermute | solution.py:754
  285.5 2.2 collective-permute-start.13
  292.5 21.3 %collective-permute-start.19 = (bf16[256,192]{1,0:T(8,128)(2,1)}, bf16[256,192]{1,0:T(8,128)(2,1)S(1)}, u32[]{:S(2)}, u32[]{:S(2)}) collective-permute-start(bf16[256,192]{1,0:T(8,128)(2,1)} %get-tuple-element.188), channel_id=1, source_target_pairs={{0,1},{1,0},{2,3},{3,2},{4,5},{5,4},{6,7},{7,6},{8,9},{9,8},{10,11... | collective-permute-start | bytes 294920 | tf_op jit(solution)/shard_map/ppermute | solution.py:754
  292.9 20.9 %collective-permute-start.20 = (bf16[256,192]{1,0:T(8,128)(2,1)}, bf16[256,192]{1,0:T(8,128)(2,1)S(1)}, u32[]{:S(2)}, u32[]{:S(2)}) collective-permute-start(bf16[256,192]{1,0:T(8,128)(2,1)} %get-tuple-element.189), channel_id=1, source_target_pairs={{0,2},{1,3},{2,0},{3,1},{4,6},{5,7},{6,4},{7,5},{8,10},{9,11},{10,... | collective-permute-start | bytes 294920 | tf_op jit(solution)/shard_map/ppermute | solution.py:754
  293.4 20.4 %collective-permute-start.21 = (bf16[256,192]{1,0:T(8,128)(2,1)}, bf16[256,192]{1,0:T(8,128)(2,1)S(1)}, u32[]{:S(2)}, u32[]{:S(2)}) collective-permute-start(bf16[256,192]{1,0:T(8,128)(2,1)} %get-tuple-element.190), channel_id=1, source_target_pairs={{0,3},{1,2},{2,1},{3,0},{4,7},{5,6},{6,5},{7,4},{8,11},{9,10},{10,... | collective-permute-start | bytes 294920 | tf_op jit(solution)/shard_map/ppermute | solution.py:754
  316.5 10.8 %copy-start.23 = (bf16[256,768]{1,0:T(8,128)(2,1)S(1)}, bf16[256,768]{1,0:T(8,128)(2,1)}, u32[]{:S(2)}) copy-start(bf16[256,768]{1,0:T(8,128)(2,1)} %get-tuple-element.175) | copy-start | bytes 1179652
  316.6 41.2 %all-to-all-start.3 = ((bf16[128,8,896]{2,1,0:T(8,128)(2,1)}), bf16[128,8,896]{2,1,0:T(8,128)(2,1)S(1)}, u32[]{:S(2)}, u32[]{:S(2)}) async-start(bf16[128,8,896]{2,1,0:T(8,128)(2,1)} %bitcast.42), calls=%async_computation.3 | async-start | bytes 3670016 | tf_op jit(solution)/shard_map/all_to_all | solution.py:746
  322.4 2.5 collective-permute-start.15
  325.0 28.8 %collective-permute-start.16 = (bf16[256,768]{1,0:T(8,128)(2,1)S(1)}, bf16[256,768]{1,0:T(8,128)(2,1)S(1)}, u32[]{:S(2)}, u32[]{:S(2)}) collective-permute-start(bf16[256,768]{1,0:T(8,128)(2,1)S(1)} %add_convert_fusion), channel_id=1, source_target_pairs={{0,2},{1,3},{2,0},{3,1},{4,6},{5,7},{6,4},{7,5},{8,10},{9,11},{10,... | collective-permute-start | bytes 1179656 | tf_op jit(solution)/shard_map/ppermute | solution.py:754
  327.3 26.5 %collective-permute-start.14 = (bf16[256,768]{1,0:T(8,128)(2,1)S(1)}, bf16[256,768]{1,0:T(8,128)(2,1)S(1)}, u32[]{:S(2)}, u32[]{:S(2)}) collective-permute-start(bf16[256,768]{1,0:T(8,128)(2,1)S(1)} %copy-done.23), channel_id=1, source_target_pairs={{0,1},{1,0},{2,3},{3,2},{4,5},{5,4},{6,7},{7,6},{8,9},{9,8},{10,11... | collective-permute-start | bytes 1179656 | tf_op jit(solution)/shard_map/ppermute | solution.py:754
  (21 other events, 50.7 us)
Sparse Core Ops, SparseCore 0:
  21.3 64.7 all-gather.6
  87.7 41.0 all-gather.8
  240.4 81.7 all-gather.10
